TPU v7x, 256 devices: a whole 4x4x8 slice. The times are simulated.
256 devices in a mesh: wide: 64 (over x, z, core), depth: 4 (over y).
Axes of the slice: x: 4, y: 4, z: 8, core: 2. Of those that a mesh axis runs over, the one named last changes fastest.
Arguments:
- amplitudes: bfloat16 [1024, 8, 1000], P('wide', 'depth'), may hold values from -6 to 6
- integrals: bfloat16 [8, 1000, 128, 1000], P('depth', None, 'wide'), may hold values from -0.1875 to 0.1875
- orbital_irrep: int32 [1000], replicated, may hold values from 0 to 7, as said below
- pair_irrep: int32 [1024], replicated, may hold values from 0 to 7
Outputs:
- ladder: bfloat16 [1024, 128, 1000], P('depth', 'wide')
Inputs may be any that keep to these rules, and one draw needn't show every extreme that they name: `orbital_irrep`: D2h irrep labels; each irrep labels at most 256 virtual orbitals, and one irrep labels exactly 256. `pair_irrep`: D2h irrep labels.
All inputs are finite; a program needn't handle non-finite values.
Results may differ from a plain program's by a relative error of at most 0.013.
Values may be sent and summed in bfloat16 or wider, within the bound.
No kernel may reach another device: no remote copies, remote signals or barrier semaphores. Data moves between devices by JAX's collectives and lax.ppermute only.
A program may use at most 128 MiB of HBM per device.

v0:
```python
import jax
import jax.numpy as jnp
from jax import lax
from jax.sharding import PartitionSpec as P


def local(amplitudes, integrals, orbital_irrep, pair_irrep):
    c_count = integrals.shape[0]
    orbitals = integrals.shape[1]
    a_count = integrals.shape[2]
    c_labels = lax.dynamic_slice_in_dim(orbital_irrep, lax.axis_index("depth") * c_count, c_count)
    a_labels = lax.dynamic_slice_in_dim(orbital_irrep, lax.axis_index("wide") * a_count, a_count)
    pair_left = jnp.bitwise_xor(c_labels[:, None], orbital_irrep[None, :])
    pair_right = jnp.bitwise_xor(a_labels[:, None], orbital_irrep[None, :])
    allowed = pair_left[:, :, None, None] == pair_right[None, None, :, :]
    masked = jnp.where(allowed, integrals, jnp.zeros((), jnp.bfloat16)).reshape(
        c_count * orbitals, a_count * orbitals
    )
    local_rows = pair_irrep.shape[0] // lax.axis_size("depth")
    local_pairs = lax.dynamic_slice_in_dim(
        pair_irrep, lax.axis_index("depth") * local_rows, local_rows
    )
    piece = lax.all_gather(amplitudes, "wide", axis=0, tiled=True)
    partial_sum = jnp.dot(
        piece.reshape(piece.shape[0], c_count * orbitals),
        masked,
        preferred_element_type=jnp.float32,
    )
    total = lax.psum_scatter(
        partial_sum.astype(jnp.bfloat16), "depth", scatter_dimension=0, tiled=True
    ).astype(jnp.float32)
    total = total.reshape(total.shape[0], a_count, orbitals)
    out_mask = local_pairs[:, None, None] == pair_right[None, :, :]
    return jnp.where(out_mask, total, 0.0).astype(jnp.bfloat16)


def solution(mesh):
    placed = (P("wide", "depth", None), P("depth", None, "wide", None), P(), P())
    return jax.shard_map(
        local, mesh=mesh, in_specs=placed, out_specs=P("depth", "wide", None), check_vma=False
    )
```

profile of v0, /device:TPU:1, one launch (start us, length us, event | category | flops | bytes accessed | tf_op | source)
XLA Modules:
  0.0 173.7 jit_solution(16328021297585863571)
XLA Ops:
  6.5 0.0 all-gather.2.cloned.1.call-start
  6.5 0.7 all-gather.2.cloned.1.call-update
  7.3 0.0 reduce-scatter.2.cloned.1.call-start
  7.3 0.8 fusion.1
  8.2 0.8 broadcast_xor_fusion
  8.9 16.9 %compare_select_fusion = bf16[2,1000,2,1000]{3,2,1,0:T(2,128)(2,1)} fusion(bf16[2,1000,2,1000]{3,2,1,0:T(2,128)(2,1)} %param.5, s32[2,1000]{1,0:T(2,128)S(1)} %get-tuple-element.6, s32[2,1000]{1,0:T(2,128)S(1)} %get-tuple-element.5), kind=kLoop, calls=%fused_computation | loop fusion | flops 8000000 | bytes 16016000 | tf_op jit(solution)/shard_map/jit(_where)/select_n | solution.py:16
  25.8 20.5 %reshape.88 = bf16[2000,2000]{1,0:T(8,128)(2,1)} reshape(bf16[2,1000,2,1000]{3,2,1,0:T(2,128)(2,1)} %compare_select_fusion) | data formatting | bytes 16000000 | tf_op jit(solution)/shard_map/reshape | solution.py:16
  46.3 47.1 %all-gather.2.cloned.1.call-done = bf16[1024,2,1000]{2,1,0:T(2,128)(2,1)} async-done(((bf16[16,2,1000]{2,1,0:T(2,128)(2,1)}), bf16[1024,2,1000]{2,1,0:T(2,128)(2,1)}) %all-gather.2.cloned.1.call-update) | async-done | bytes 4096016 | tf_op jit(solution)/shard_map/all_gather | solution.py:23
  93.4 11.2 %copy.6 = bf16[1024,2,1000]{0,2,1:T(8,128)(2,1)} copy(bf16[1024,2,1000]{2,1,0:T(2,128)(2,1)} %all-gather.2.cloned.1.call-done) | data formatting | bytes 8192000 | tf_op jit(solution)/shard_map/all_gather | solution.py:23
  104.6 14.3 %convert_bitcast_fusion = bf16[1024,2000]{0,1:T(8,128)(2,1)} fusion(bf16[2000,2000]{1,0:T(8,128)(2,1)} %reshape.88, bf16[1024,2000]{0,1:T(8,128)(2,1)} %bitcast.7), kind=kOutput, calls=%fused_computation.1 | convolution fusion | flops 8194048000 | bytes 16192000 | tf_op jit(solution)/shard_map/dot_general | solution.py:24
  118.9 0.0 reduce-scatter.2.cloned.1.call-update
  118.9 0.8 dynamic_slice.9
  119.7 44.9 %reduce-scatter.2.cloned.1.call-done = bf16[256,2000]{0,1:T(8,128)(2,1)} async-done(((bf16[1024,2000]{0,1:T(8,128)(2,1)}), bf16[256,2000]{0,1:T(8,128)(2,1)}) %reduce-scatter.2.cloned.1.call-update) | async-done | bytes 1024016 | tf_op jit(solution)/shard_map/reduce_scatter | solution.py:29
  164.6 2.2 %fusion = bf16[256,2,1000]{0,2,1:T(8,128)(2,1)} fusion(bf16[256,2,1000]{0,2,1:T(8,128)(2,1)} %bitcast.8, s32[2,1000]{1,0:T(2,128)S(1)} %get-tuple-element.6, s32[256]{0:T(256)S(1)} %dynamic_slice.9), kind=kLoop, calls=%fused_computation.3 | loop fusion | flops 2048000 | bytes 2057024 | tf_op jit(solution)/shard_map/convert_element_type | solution.py:34
Async XLA Ops:
  6.5 86.8 %all-gather.2.cloned.1.call-start = ((), (), s32[]{:S(2)}) async-start(), calls=%async_computation.1 | async-start | bytes 4259840 | tf_op jit(solution)/shard_map/all_gather | solution.py:23
  7.3 157.3 %reduce-scatter.2.cloned.1.call-start = ((), (), s32[]{:S(2)}) async-start(), calls=%async_computation.2 | async-start | bytes 5120000 | tf_op jit(solution)/shard_map/reduce_scatter | solution.py:29
Sparse Core Ops, SparseCore 0:
  10.1 83.1 all-gather.1
  119.0 45.5 reduce-scatter.1
where the time goes:
time: 175 us; the launch traced here: 174 us
  waiting for transfers between devices  92.7 us (53%)
  local copies, waits for them, and re-layouts  33.3 us (19%)
  other arithmetic  19.9 us (11%)
  matrix products  14.3 us (8%)
  between operations  13.4 us (8%)
    all_gather x1, waiting for transfers between devices, local(): piece = lax.all_gather(amplitudes, 'wide', axis=0, tiled=True)  47.1 us
    reduce_scatter x1, waiting for transfers between devices, local(): lax.psum_scatter(partial_sum.astype(jnp.bfloat16), 'depth', scatter_dimen...  44.9 us
    reshape x1, local copies, waits for them, and re-layouts, local(): jnp.where(allowed, integrals, jnp.zeros((), jnp.bfloat16))  20.5 us
    select_n x1, other arithmetic, local(): jnp.where(allowed, integrals, jnp.zeros((), jnp.bfloat16))  16.9 us
    dot_general x1, matrix products, local(): jnp.dot(piece.reshape(piece.shape[0], c_count * orbitals), masked, prefer...  14.3 us
    all_gather x1, local copies, waits for them, and re-layouts, local(): piece = lax.all_gather(amplitudes, 'wide', axis=0, tiled=True)  11.2 us
  transfers between devices with their start and end apart: 2, of which 2 were waited for; matrix products, arithmetic and copies ran while one was open for 23% of the time, Pallas kernels for 0%

commit v1 on v0

v1 whole, which is shorter than its diff:
```python
import functools

import jax
import jax.numpy as jnp
from jax import lax
from jax.experimental import pallas as pl
from jax.experimental.pallas import tpu as pltpu
from jax.sharding import PartitionSpec as P

SLOTS = 256
NX, NZ, NC, NY = 4, 8, 2, 4
BF, F32, I32 = jnp.bfloat16, jnp.float32, jnp.int32
LO, HI = (0, 1, -1, 2), (-2, 3, -3, 4)
VMEM = pl.BlockSpec(memory_space=pltpu.VMEM)
ANY = pl.BlockSpec(memory_space=pl.ANY)


def coords():
    w = lax.axis_index("wide")
    return w // (NZ * NC), (w // NC) % NZ, w % NC, lax.axis_index("depth")


def pick(row, index):
    lane = lax.broadcasted_iota(I32, row.shape, 1)
    return jnp.sum(jnp.where(lane == index, row, 0), axis=1, keepdims=True)


def pack_matrix(slot):
    row = lax.broadcasted_iota(I32, (SLOTS, slot.shape[1]), 0)
    return jnp.where(row == slot, 1.0, 0.0).astype(BF)


def nt(left, right):
    return lax.dot_general(left, right, (((1,), (1,)), ((), ())), preferred_element_type=F32)


def compact_kernel(t_ref, orb_ref, pair_ref, packed_ref, slot_ref):
    x, z, core, y = coords()
    w = (x * NZ + z) * NC + core
    rows, c_count, n = t_ref.shape
    orb = orb_ref[...]
    member = jnp.where(lax.broadcasted_iota(I32, (8, n), 0) == orb, 1.0, 0.0)
    upto = jnp.where(
        lax.broadcasted_iota(I32, (128, 128), 0) <= lax.broadcasted_iota(I32, (128, 128), 1), 1.0, 0.0
    ).astype(BF)
    before = jnp.zeros((8, 1), F32)
    counts = []
    for start in range(0, n, 128):
        size = min(128, n - start)
        part = member[:, start:start + size]
        counts.append(jnp.dot(part.astype(BF), upto[:size, :size], preferred_element_type=F32) + before)
        before = before + jnp.sum(part, axis=1, keepdims=True)
    count = jnp.concatenate(counts, axis=1)
    slot = jnp.sum(member * count, axis=0, keepdims=True).astype(I32) - 1
    slot_ref[...] = slot
    onehot = pack_matrix(slot)
    pair = pair_ref[...]
    lane = lax.broadcasted_iota(I32, (rows, pair.shape[1]), 1)
    row = lax.broadcasted_iota(I32, (rows, pair.shape[1]), 0)
    pair_col = jnp.sum(jnp.where(lane == row + w * rows, pair, 0), axis=1, keepdims=True)
    amps = t_ref[...]
    for c in range(c_count):
        label = pick(orb, y * c_count + c)
        kept = jnp.where(orb == (pair_col ^ label), amps[:, c, :].astype(F32), 0.0).astype(BF)
        packed_ref[c] = nt(kept, onehot).astype(BF)


def compact(amplitudes, orb, pair):
    rows, c_count, n = amplitudes.shape
    return pl.pallas_call(
        compact_kernel,
        out_shape=(
            jax.ShapeDtypeStruct((c_count, rows, SLOTS), BF),
            jax.ShapeDtypeStruct((1, n), I32),
        ),
        in_specs=[VMEM] * 3,
        out_specs=(VMEM, VMEM),
        name="compact",
    )(amplitudes, orb, pair)


def column(row):
    return jnp.transpose(jnp.broadcast_to(row, (8, row.shape[1])))[:, :1]


def partial_kernel(offsets, a_list, add_at, final, *refs):
    n_add = len(add_at)
    blocks = refs[:16]
    v_ref, orb_ref, pair_ref, slot_ref = refs[16:20]
    adds = refs[20:20 + n_add]
    out_ref = refs[20 + n_add]
    held, spread, acc, sem = refs[21 + n_add:]
    x, z, core, y = coords()
    ai, c = pl.program_id(0), pl.program_id(1)
    n = orb_ref.shape[1]
    rows = NZ * NC * 16
    w = (x * NZ + z) * NC + core
    orb = orb_ref[...]
    dests = [lax.rem(y + off, NY) for off in offsets]

    def pair_of(dest):
        pair = pair_ref[...]
        total = jnp.zeros((1, rows), I32)
        for k in range(NY):
            total = total + jnp.where(dest == k, pair[:, rows * k:rows * (k + 1)], 0)
        return total

    pair_col = jnp.concatenate([column(pair_of(dest)) for dest in dests], axis=0)

    @pl.when((ai == 0) & (c == 0))
    def _():
        onehot = pack_matrix(slot_ref[...])
        for i, dest in enumerate(dests):
            rel = lax.rem(dest - x + NX, NX)
            for k in range(NX):
                @pl.when(rel == k)
                def _():
                    for j in range(4):
                        pltpu.make_async_copy(blocks[4 * k + j], held.at[i, j], sem.at[i, j]).start()
        for i, dest in enumerate(dests):
            for j in range(4):
                pltpu.make_async_copy(blocks[j], held.at[i, j], sem.at[i, j]).wait()
            for cc in range(2):
                parts = [None] * 16
                label = pick(orb, y * 2 + cc)
                for half, order in enumerate((LO, HI)):
                    for b, dz in enumerate(order):
                        zz = lax.rem(z + dz + NZ, NZ)
                        for other in range(NC):
                            at = zz * (NC * 16) + lax.rem(core + other, NC) * 16
                            spread[cc, pl.ds(pl.multiple_of(i * rows + at, 16), 16), :SLOTS] = held[
                                i, half * 2 + other, b, cc
                            ]
        for cc in range(2):
            label = pick(orb, y * 2 + cc)
            full = jnp.dot(spread[cc, :, :SLOTS], onehot, preferred_element_type=F32)
            spread[cc] = jnp.where(orb == (pair_col ^ label), full, 0.0).astype(BF)

    @pl.when(c == 0)
    def _():
        acc[...] = jnp.dot(spread[0], v_ref[0], preferred_element_type=F32)

    @pl.when(c == 1)
    def _():
        total = acc[...] + jnp.dot(spread[1], v_ref[0], preferred_element_type=F32)
        onehot = pack_matrix(slot_ref[...])
        for k, a in enumerate(a_list):
            @pl.when(ai == k)
            def _():
                label = pick(orb, w * 2 + a)
                kept = jnp.where(orb == (pair_col ^ label), total, 0.0).astype(BF)
                packed = nt(onehot, kept)
                for i in range(len(offsets)):
                    value = packed[:, i * rows:(i + 1) * rows]
                    for m, (off, aa) in enumerate(add_at):
                        if off == offsets[i] and aa == a:
                            value = value + adds[m][...].astype(F32)
                    if final:
                        for m, (off, aa) in enumerate(add_at):
                            if off is None and aa == a:
                                value = value + adds[m][...].astype(F32)
                        full = lax.dot_general(
                            onehot, value.astype(BF), (((0,), (0,)), ((), ())), preferred_element_type=F32
                        )
                        orb_col = column(orb)
                        keep = orb_col == (pair_of(dests[0]) ^ label)
                        out_ref[0] = jnp.where(keep, full, 0.0).astype(BF)
                    else:
                        out_ref[k * len(offsets) + i] = value.astype(BF)


def partial(blocks, v, orb, pair, slot, offsets, a_list, add_at=(), adds=(), final=False):
    n = orb.shape[1]
    rows = NZ * NC * 16
    chunk_rows = rows * len(offsets)
    if final:
        out_shape = jax.ShapeDtypeStruct((2, n, rows), BF)
        out_spec = pl.BlockSpec((1, n, rows), lambda a, c: (a, 0, 0))
    else:
        out_shape = jax.ShapeDtypeStruct((len(a_list) * len(offsets), SLOTS, rows), BF)
        out_spec = VMEM
    first = a_list[0]
    whole = lambda array: pl.BlockSpec(array.shape, lambda a, c: (0,) * array.ndim)
    flops = 2 * chunk_rows * n * n * 2 * len(a_list)
    return pl.pallas_call(
        functools.partial(partial_kernel, offsets, a_list, add_at, final),
        grid=(len(a_list), 2),
        out_shape=out_shape,
        in_specs=[ANY] * 16
        + [pl.BlockSpec((1, n, n), lambda a, c: ((a + first) * 2 + c, 0, 0))]
        + [whole(orb), whole(pair), whole(slot)]
        + [whole(add) for add in adds],
        out_specs=out_spec,
        scratch_shapes=[
            pltpu.VMEM((len(offsets), 4, 4, 2, 16, SLOTS), BF),
            pltpu.VMEM((2, chunk_rows, n), BF),
            pltpu.VMEM((chunk_rows, n), F32),
            pltpu.SemaphoreType.DMA((len(offsets), 4)),
        ],
        compiler_params=pltpu.CompilerParams(vmem_limit_bytes=40 << 20),
        cost_estimate=pl.CostEstimate(flops=flops, bytes_accessed=4 * n * n * len(a_list), transcendentals=0),
        name="partial",
    )(*blocks, v, orb, pair, slot, *adds)


def wide_perm(dx, dz, dc):
    index = lambda x, z, c: (x % NX * NZ + z % NZ) * NC + c % NC
    return [
        (index(x + dx, z + dz, c + dc), index(x, z, c)) for x in range(NX) for z in range(NZ) for c in range(NC)
    ]


def from_wide(value, dx=0, dz=0, dc=0):
    return lax.ppermute(value, "wide", wide_perm(dx, dz, dc))


def to_depth(value, dy):
    return lax.ppermute(value, "depth", [(i, (i + dy) % NY) for i in range(NY)])


def gather(block):
    at = {0: block}
    for step in range(1, 5):
        at[step] = from_wide(at[step - 1], dz=1)
        if step < 4:
            at[-step] = from_wide(at[1 - step], dz=-1)
    low = jnp.stack([at[k] for k in LO])
    high = jnp.stack([at[k] for k in HI])
    lows, highs = {0: low}, {0: high}
    for dx in (1, -1):
        lows[dx] = from_wide(low, dx=dx)
        highs[dx] = from_wide(high, dx=dx)
    lows[2] = from_wide(lows[1], dx=1)
    highs[2] = from_wide(highs[-1], dx=-1)
    out = []
    for dx in (0, 1, 2, -1):
        for value in (lows[dx], highs[dx]):
            out += [value, from_wide(value, dc=1)]
    return out


def local(amplitudes, integrals, orbital_irrep, pair_irrep):
    c_count, n, a_count, _ = integrals.shape
    orb = orbital_irrep.reshape(1, n)
    pair = pair_irrep.reshape(1, pair_irrep.shape[0])
    v = jnp.transpose(integrals, (2, 0, 1, 3)).reshape(a_count * c_count, n, n)
    packed, slot = compact(amplitudes, orb, pair)
    blocks = gather(packed)
    call = functools.partial(partial, blocks, v, orb, pair, slot)
    far = call((2,), (0, 1))
    far_up = to_depth(far[0], 1)
    far_down = to_depth(far[1], -1)
    mid0 = call((1, 3), (0,), ((1, 0),), (far_up,))
    up0, down0 = to_depth(mid0[0], 1), to_depth(mid0[1], -1)
    mid1 = call((1, 3), (1,), ((3, 1),), (far_down,))
    up1, down1 = to_depth(mid1[0], 1), to_depth(mid1[1], -1)
    out = call(
        (0,), (0, 1), ((None, 0), (None, 0), (None, 1), (None, 1)), (up0, down0, up1, down1), final=True
    )
    return jnp.transpose(out, (2, 0, 1))


def solution(mesh):
    placed = (P("wide", "depth", None), P("depth", None, "wide", None), P(), P())
    return jax.shard_map(
        local, mesh=mesh, in_specs=placed, out_specs=P("depth", "wide", None), check_vma=False
    )
```

time: 175 us -> 94.6 us (0.54)
  waiting for transfers between devices: 92.7 us -> 11.7 us
  starting transfers between devices: 0.04 us -> 41.2 us
  Pallas kernels: 0 us -> 26.7 us
  local copies, waits for them, and re-layouts: 33.3 us -> 13.3 us
  other arithmetic: 19.9 us -> 0.74 us
  matrix products: 14.3 us -> 0 us
  between operations: 13.4 us -> 0.37 us
    all_gather x1 -> x0, waiting for transfers between devices: 47.1 us -> none  [local(): piece = lax.all_gather(amplitudes, 'wide', axis=0, tiled=True)]
    reduce_scatter x1 -> x0, waiting for transfers between devices: 44.9 us -> none  [local(): lax.psum_scatter(partial_sum.astype(jnp.bfloat16), 'depth', scatter_dimen...]
    ppermute x0 -> x27, starting transfers between devices: none -> 41.2 us  [the longest x21 31.5 us: from_wide(): return lax.ppermute(value, 'wide', wide_perm(dx, dz, dc))]
    pallas_call x0 -> x5, Pallas kernels: none -> 26.7 us  [the longest x4 24.7 us: partial(): pl.pallas_call(functools.partial(partial_kernel, offsets, a_list, add_at,...]
    reshape x1 -> x0, local copies, waits for them, and re-layouts: 20.5 us -> none  [local(): jnp.where(allowed, integrals, jnp.zeros((), jnp.bfloat16))]
    select_n x1 -> x0, other arithmetic: 16.9 us -> none  [local(): jnp.where(allowed, integrals, jnp.zeros((), jnp.bfloat16))]
    dot_general x1 -> x0, matrix products: 14.3 us -> none  [local(): jnp.dot(piece.reshape(piece.shape[0], c_count * orbitals), masked, prefer...]
    ppermute x0 -> x27, waiting for transfers between devices: none -> 11.7 us  [the longest x6 7.95 us: to_depth(): return lax.ppermute(value, 'depth', [(i, (i + dy) % NY) for i in range(NY)])]
  transfers between devices with their start and end apart: 2 -> 27, of which waited for: 2 -> 7; matrix products, arithmetic and copies ran while one was open for 23% -> 7% of each run, Pallas kernels for 0% -> 11%
where the time goes in v1:
time: 94.6 us; the launch traced here: 94 us
  starting transfers between devices  41.2 us (44%)
  Pallas kernels  26.7 us (28%)
  local copies, waits for them, and re-layouts  13.3 us (14%)
  waiting for transfers between devices  11.7 us (12%)
    ppermute x21, starting transfers between devices, from_wide(): return lax.ppermute(value, 'wide', wide_perm(dx, dz, dc))  31.5 us
    pallas_call x4, Pallas kernels, partial(): pl.pallas_call(functools.partial(partial_kernel, offsets, a_list, add_at,...  24.7 us
    ppermute x6, starting transfers between devices, to_depth(): return lax.ppermute(value, 'depth', [(i, (i + dy) % NY) for i in range(NY)])  9.73 us
    ppermute x6, waiting for transfers between devices, to_depth(): return lax.ppermute(value, 'depth', [(i, (i + dy) % NY) for i in range(NY)])  7.95 us
    unnamed x26, local copies, waits for them, and re-layouts  7.3 us
    transpose x1, local copies, waits for them, and re-layouts, local(): v = jnp.transpose(integrals, (2, 0, 1, 3)).reshape(a_count * c_count, n, n)  5.97 us
    ppermute x21, waiting for transfers between devices, from_wide(): return lax.ppermute(value, 'wide', wide_perm(dx, dz, dc))  3.73 us
    pallas_call x1, Pallas kernels, compact(): pl.pallas_call(compact_kernel, out_shape=(jax.ShapeDtypeStruct((c_count,...  2 us
  transfers between devices with their start and end apart: 27, of which 7 were waited for; matrix products, arithmetic and copies ran while one was open for 7% of the time, Pallas kernels for 11%

profile of v1, /device:TPU:1, one launch (start us, length us, event | category | flops | bytes accessed | tf_op | source)
XLA Modules:
  0.0 94.0 jit_solution(12504329694122655180)
XLA Ops:
  0.0 2.0 %compact.1 = (bf16[2,16,256]{2,1,0:T(8,128)(2,1)}, s32[1,1000]{1,0:T(1,128)}) custom-call(bf16[16,2,1000]{2,1,0:T(2,128)(2,1)} %t_ref.1, s32[1,1000]{1,0:T(1,128)} %bitcast.29, s32[1,1024]{1,0:T(1,128)} %bitcast.34), custom_call_target="tpu_custom_call" | custom-call | tf_op jit(solution)/shard_map/compact/pallas_call | solution.py:70
  2.0 6.4 %collective-permute-start = (bf16[2,16,256]{2,1,0:T(8,128)(2,1)}, bf16[2,16,256]{2,1,0:T(8,128)(2,1)S(1)}, u32[]{:S(2)}, u32[]{:S(2)}) collective-permute-start(bf16[2,16,256]{2,1,0:T(8,128)(2,1)} %get-tuple-element.7), channel_id=1, source_target_pairs={{8,0},{12,4},{16,8},{20,12},{24,16},{28,20},{32,24},{36,28},{40,32... | collective-permute-start | bytes 49160 | tf_op jit(solution)/shard_map/ppermute | solution.py:214
  8.4 1.1 %collective-permute-done = bf16[2,16,256]{2,1,0:T(8,128)(2,1)S(1)} collective-permute-done((bf16[2,16,256]{2,1,0:T(8,128)(2,1)}, bf16[2,16,256]{2,1,0:T(8,128)(2,1)S(1)}, u32[]{:S(2)}, u32[]{:S(2)}) %collective-permute-start) | collective-permute-done | bytes 16416 | tf_op jit(solution)/shard_map/ppermute | solution.py:214
  9.5 2.9 %collective-permute-start.2 = (bf16[2,16,256]{2,1,0:T(8,128)(2,1)S(1)}, bf16[2,16,256]{2,1,0:T(8,128)(2,1)S(1)}, u32[]{:S(2)}, u32[]{:S(2)}) collective-permute-start(bf16[2,16,256]{2,1,0:T(8,128)(2,1)S(1)} %collective-permute-done), channel_id=1, source_target_pairs={{8,0},{12,4},{16,8},{20,12},{24,16},{28,20},{32,24},{36,28},{40,32... | collective-permute-start | bytes 49160 | tf_op jit(solution)/shard_map/ppermute | solution.py:214
  13.3 2.9 %collective-permute-start.5 = (bf16[2,16,256]{2,1,0:T(8,128)(2,1)S(1)}, bf16[2,16,256]{2,1,0:T(8,128)(2,1)S(1)}, u32[]{:S(2)}, u32[]{:S(2)}) collective-permute-start(bf16[2,16,256]{2,1,0:T(8,128)(2,1)S(1)} %collective-permute-done.2), channel_id=1, source_target_pairs={{8,0},{12,4},{16,8},{20,12},{24,16},{28,20},{32,24},{36,28},{40,32... | collective-permute-start | bytes 49160 | tf_op jit(solution)/shard_map/ppermute | solution.py:214
  17.1 2.9 %collective-permute-start.7 = (bf16[2,16,256]{2,1,0:T(8,128)(2,1)S(1)}, bf16[2,16,256]{2,1,0:T(8,128)(2,1)S(1)}, u32[]{:S(2)}, u32[]{:S(2)}) collective-permute-start(bf16[2,16,256]{2,1,0:T(8,128)(2,1)S(1)} %collective-permute-done.5), channel_id=1, source_target_pairs={{8,0},{12,4},{16,8},{20,12},{24,16},{28,20},{32,24},{36,28},{40,32... | collective-permute-start | bytes 49160 | tf_op jit(solution)/shard_map/ppermute | solution.py:214
  20.7 1.3 %collective-permute-start.18 = (bf16[4,2,16,256]{3,2,1,0:T(8,128)(2,1)S(1)}, bf16[4,2,16,256]{3,2,1,0:T(8,128)(2,1)S(1)}, u32[]{:S(2)}, u32[]{:S(2)}) collective-permute-start(bf16[4,2,16,256]{3,2,1,0:T(8,128)(2,1)S(1)} %pad_maximum_fusion.refs_0_), channel_id=1, source_target_pairs={{192,0},{196,4},{200,8},{204,12},{208,16},{212,20},{216,24},{220,2... | collective-permute-start | bytes 196616 | tf_op jit(solution)/shard_map/ppermute | solution.py:214
  22.0 1.5 %collective-permute-start.9 = (bf16[4,2,16,256]{3,2,1,0:T(8,128)(2,1)S(1)}, bf16[4,2,16,256]{3,2,1,0:T(8,128)(2,1)}, u32[]{:S(2)}, u32[]{:S(2)}) collective-permute-start(bf16[4,2,16,256]{3,2,1,0:T(8,128)(2,1)S(1)} %pad_maximum_fusion.refs_0_), channel_id=1, source_target_pairs={{64,0},{68,4},{72,8},{76,12},{80,16},{84,20},{88,24},{92,28},{96,3... | collective-permute-start | bytes 196616 | tf_op jit(solution)/shard_map/ppermute | solution.py:214
  23.5 5.0 %collective-permute-start.3 = (bf16[4,2,16,256]{3,2,1,0:T(8,128)(2,1)S(1)}, bf16[4,2,16,256]{3,2,1,0:T(8,128)(2,1)S(1)}, u32[]{:S(2)}, u32[]{:S(2)}) collective-permute-start(bf16[4,2,16,256]{3,2,1,0:T(8,128)(2,1)S(1)} %pad_maximum_fusion.refs_0_), channel_id=1, source_target_pairs={{4,0},{0,4},{12,8},{8,12},{20,16},{16,20},{28,24},{24,28},{36,32},... | collective-permute-start | bytes 196616 | tf_op jit(solution)/shard_map/ppermute | solution.py:214
  28.6 2.7 %collective-permute-start.11 = (bf16[4,2,16,256]{3,2,1,0:T(8,128)(2,1)S(1)}, bf16[4,2,16,256]{3,2,1,0:T(8,128)(2,1)}, u32[]{:S(2)}, u32[]{:S(2)}) collective-permute-start(bf16[4,2,16,256]{3,2,1,0:T(8,128)(2,1)S(1)} %pad_maximum_fusion.1.refs_2_), channel_id=1, source_target_pairs={{64,0},{68,4},{72,8},{76,12},{80,16},{84,20},{88,24},{92,28},{96,3... | collective-permute-start | bytes 196616 | tf_op jit(solution)/shard_map/ppermute | solution.py:214
  33.7 1.3 %collective-permute-start.13 = (bf16[4,2,16,256]{3,2,1,0:T(8,128)(2,1)}, bf16[4,2,16,256]{3,2,1,0:T(8,128)(2,1)}, u32[]{:S(2)}, u32[]{:S(2)}) collective-permute-start(bf16[4,2,16,256]{3,2,1,0:T(8,128)(2,1)} %collective-permute-done.9.refs_4_), channel_id=1, source_target_pairs={{64,0},{68,4},{72,8},{76,12},{80,16},{84,20},{88,24},{92,28},{96,3... | collective-permute-start | bytes 196616 | tf_op jit(solution)/shard_map/ppermute | solution.py:214
  35.2 1.1 %collective-permute-start.10 = (bf16[4,2,16,256]{3,2,1,0:T(8,128)(2,1)}, bf16[4,2,16,256]{3,2,1,0:T(8,128)(2,1)}, u32[]{:S(2)}, u32[]{:S(2)}) collective-permute-start(bf16[4,2,16,256]{3,2,1,0:T(8,128)(2,1)} %collective-permute-done.9.refs_4_), channel_id=1, source_target_pairs={{4,0},{0,4},{12,8},{8,12},{20,16},{16,20},{28,24},{24,28},{36,32},... | collective-permute-start | bytes 196616 | tf_op jit(solution)/shard_map/ppermute | solution.py:214
  39.7 1.4 %collective-permute-start.17 = (bf16[4,2,16,256]{3,2,1,0:T(8,128)(2,1)}, bf16[4,2,16,256]{3,2,1,0:T(8,128)(2,1)}, u32[]{:S(2)}, u32[]{:S(2)}) collective-permute-start(bf16[4,2,16,256]{3,2,1,0:T(8,128)(2,1)} %collective-permute-done.16.refs_10_), channel_id=1, source_target_pairs={{4,0},{0,4},{12,8},{8,12},{20,16},{16,20},{28,24},{24,28},{36,32},... | collective-permute-start | bytes 196616 | tf_op jit(solution)/shard_map/ppermute | solution.py:214
  41.1 6.0 %copy.5 = bf16[2,2,1000,1000]{3,2,1,0:T(8,128)(2,1)S(1)} copy(bf16[2,2,1000,1000]{3,0,2,1:T(2,128)(2,1)} %bitcast.39) | data formatting | bytes 16000000 | tf_op jit(solution)/shard_map/transpose | solution.py:246
  51.4 6.3 %partial.4 = bf16[2,256,256]{2,1,0:T(8,128)(2,1)S(1)} custom-call(bf16[4,2,16,256]{3,2,1,0:T(8,128)(2,1)S(1)} %pad_maximum_fusion.refs_0_, bf16[4,2,16,256]{3,2,1,0:T(8,128)(2,1)S(1)} %copy-done.5, bf16[4,2,16,256]{3,2,1,0:T(8,128)(2,1)S(1)} %copy-done.1, bf16[4,2,16,256]{3,2,1,0:T(8,128)(2,1)S(1)} %copy-done.7, ...), custom_call_target="tpu_custom_call" | custom-call | flops 2048000000 | bytes 8000000 | tf_op jit(solution)/shard_map/partial/pallas_call | solution.py:185
  57.7 2.8 %collective-permute-start.24 = (bf16[256,256]{1,0:T(8,128)(2,1)S(1)}, bf16[256,256]{1,0:T(8,128)(2,1)S(1)}, u32[]{:S(2)}, u32[]{:S(2)}) collective-permute-start(bf16[256,256]{1,0:T(8,128)(2,1)S(1)} %get-tuple-element.11), channel_id=1, source_target_pairs={{0,3},{1,0},{2,1},{3,2},{4,7},{5,4},{6,5},{7,6},{8,11},{9,8},{10,9... | collective-permute-start | bytes 393224 | tf_op jit(solution)/shard_map/ppermute | solution.py:218
  60.5 2.9 %collective-permute-done.24.refs_20_ = bf16[256,256]{1,0:T(8,128)(2,1)S(1)} collective-permute-done((bf16[256,256]{1,0:T(8,128)(2,1)S(1)}, bf16[256,256]{1,0:T(8,128)(2,1)S(1)}, u32[]{:S(2)}, u32[]{:S(2)}) %collective-permute-start.24) | collective-permute-done | bytes 131104 | tf_op jit(solution)/shard_map/ppermute | solution.py:218
  63.4 5.2 %partial.6 = bf16[2,256,256]{2,1,0:T(8,128)(2,1)S(1)} custom-call(bf16[4,2,16,256]{3,2,1,0:T(8,128)(2,1)S(1)} %pad_maximum_fusion.refs_0_, bf16[4,2,16,256]{3,2,1,0:T(8,128)(2,1)S(1)} %copy-done.5, bf16[4,2,16,256]{3,2,1,0:T(8,128)(2,1)S(1)} %copy-done.1, bf16[4,2,16,256]{3,2,1,0:T(8,128)(2,1)S(1)} %copy-done.7, ...), custom_call_target="tpu_custom_call" | custom-call | flops 2048000000 | bytes 4000000 | tf_op jit(solution)/shard_map/partial/pallas_call | solution.py:185
  68.7 3.9 %collective-permute-start.26 = (bf16[256,256]{1,0:T(8,128)(2,1)S(1)}, bf16[256,256]{1,0:T(8,128)(2,1)S(1)}, u32[]{:S(2)}, u32[]{:S(2)}) collective-permute-start(bf16[256,256]{1,0:T(8,128)(2,1)S(1)} %get-tuple-element.9), channel_id=1, source_target_pairs={{0,3},{1,0},{2,1},{3,2},{4,7},{5,4},{6,5},{7,6},{8,11},{9,8},{10,9... | collective-permute-start | bytes 393224 | tf_op jit(solution)/shard_map/ppermute | solution.py:218
  72.7 5.3 %partial.5 = bf16[2,256,256]{2,1,0:T(8,128)(2,1)S(1)} custom-call(bf16[4,2,16,256]{3,2,1,0:T(8,128)(2,1)S(1)} %pad_maximum_fusion.refs_0_, bf16[4,2,16,256]{3,2,1,0:T(8,128)(2,1)S(1)} %copy-done.5, bf16[4,2,16,256]{3,2,1,0:T(8,128)(2,1)S(1)} %copy-done.1, bf16[4,2,16,256]{3,2,1,0:T(8,128)(2,1)S(1)} %copy-done.7, ...), custom_call_target="tpu_custom_call" | custom-call | flops 2048000000 | bytes 4000000 | tf_op jit(solution)/shard_map/partial/pallas_call | solution.py:185
  78.0 3.0 %collective-permute-start.23 = (bf16[256,256]{1,0:T(8,128)(2,1)S(1)}, bf16[256,256]{1,0:T(8,128)(2,1)S(1)}, u32[]{:S(2)}, u32[]{:S(2)}) collective-permute-start(bf16[256,256]{1,0:T(8,128)(2,1)S(1)} %get-tuple-element.13), channel_id=1, source_target_pairs={{0,3},{1,0},{2,1},{3,2},{4,7},{5,4},{6,5},{7,6},{8,11},{9,8},{10,9... | collective-permute-start | bytes 393224 | tf_op jit(solution)/shard_map/ppermute | solution.py:218
  80.9 1.9 %collective-permute-done.23.refs_21_ = bf16[256,256]{1,0:T(8,128)(2,1)S(1)} collective-permute-done((bf16[256,256]{1,0:T(8,128)(2,1)S(1)}, bf16[256,256]{1,0:T(8,128)(2,1)S(1)}, u32[]{:S(2)}, u32[]{:S(2)}) %collective-permute-start.23) | collective-permute-done | bytes 131104 | tf_op jit(solution)/shard_map/ppermute | solution.py:218
  82.9 3.1 %collective-permute-done.22.refs_20_ = bf16[256,256]{1,0:T(8,128)(2,1)S(1)} collective-permute-done((bf16[256,256]{1,0:T(8,128)(2,1)S(1)}, bf16[256,256]{1,0:T(8,128)(2,1)S(1)}, u32[]{:S(2)}, u32[]{:S(2)}) %collective-permute-start.22) | collective-permute-done | bytes 131104 | tf_op jit(solution)/shard_map/ppermute | solution.py:218
  86.0 7.9 %partial.7 = bf16[2,1000,256]{2,1,0:T(8,128)(2,1)} custom-call(bf16[4,2,16,256]{3,2,1,0:T(8,128)(2,1)S(1)} %pad_maximum_fusion.refs_0_, bf16[4,2,16,256]{3,2,1,0:T(8,128)(2,1)S(1)} %copy-done.5, bf16[4,2,16,256]{3,2,1,0:T(8,128)(2,1)S(1)} %copy-done.1, bf16[4,2,16,256]{3,2,1,0:T(8,128)(2,1)S(1)} %copy-done.7, ...), custom_call_target="tpu_custom_call" | custom-call | flops 2048000000 | bytes 8000000 | tf_op jit(solution)/shard_map/partial/pallas_call | solution.py:185
  (67 shorter events, 12.9 us)
Async XLA Ops:
  2.0 7.5 %collective-permute-start = (bf16[2,16,256]{2,1,0:T(8,128)(2,1)}, bf16[2,16,256]{2,1,0:T(8,128)(2,1)S(1)}, u32[]{:S(2)}, u32[]{:S(2)}) collective-permute-start(bf16[2,16,256]{2,1,0:T(8,128)(2,1)} %get-tuple-element.7), channel_id=1, source_target_pairs={{8,0},{12,4},{16,8},{20,12},{24,16},{28,20},{32,24},{36,28},{40,32... | collective-permute-start | bytes 49160 | tf_op jit(solution)/shard_map/ppermute | solution.py:214
  8.4 4.0 %collective-permute-start.1 = (bf16[2,16,256]{2,1,0:T(8,128)(2,1)}, bf16[2,16,256]{2,1,0:T(8,128)(2,1)S(1)}, u32[]{:S(2)}, u32[]{:S(2)}) collective-permute-start(bf16[2,16,256]{2,1,0:T(8,128)(2,1)} %get-tuple-element.7), channel_id=1, source_target_pairs={{56,0},{60,4},{0,8},{4,12},{8,16},{12,20},{16,24},{20,28},{24,32},... | collective-permute-start | bytes 49160 | tf_op jit(solution)/shard_map/ppermute | solution.py:214
  16.2 12.2 %collective-permute-start.6 = (bf16[2,16,256]{2,1,0:T(8,128)(2,1)S(1)}, bf16[2,16,256]{2,1,0:T(8,128)(2,1)S(1)}, u32[]{:S(2)}, u32[]{:S(2)}) collective-permute-start(bf16[2,16,256]{2,1,0:T(8,128)(2,1)S(1)} %collective-permute-done.4), channel_id=1, source_target_pairs={{56,0},{60,4},{0,8},{4,12},{8,16},{12,20},{16,24},{20,28},{24,32},... | collective-permute-start | bytes 49160 | tf_op jit(solution)/shard_map/ppermute | solution.py:214
  17.1 11.4 %collective-permute-start.7 = (bf16[2,16,256]{2,1,0:T(8,128)(2,1)S(1)}, bf16[2,16,256]{2,1,0:T(8,128)(2,1)S(1)}, u32[]{:S(2)}, u32[]{:S(2)}) collective-permute-start(bf16[2,16,256]{2,1,0:T(8,128)(2,1)S(1)} %collective-permute-done.5), channel_id=1, source_target_pairs={{8,0},{12,4},{16,8},{20,12},{24,16},{28,20},{32,24},{36,28},{40,32... | collective-permute-start | bytes 49160 | tf_op jit(solution)/shard_map/ppermute | solution.py:214
  20.7 10.5 %collective-permute-start.18 = (bf16[4,2,16,256]{3,2,1,0:T(8,128)(2,1)S(1)}, bf16[4,2,16,256]{3,2,1,0:T(8,128)(2,1)S(1)}, u32[]{:S(2)}, u32[]{:S(2)}) collective-permute-start(bf16[4,2,16,256]{3,2,1,0:T(8,128)(2,1)S(1)} %pad_maximum_fusion.refs_0_), channel_id=1, source_target_pairs={{192,0},{196,4},{200,8},{204,12},{208,16},{212,20},{216,24},{220,2... | collective-permute-start | bytes 196616 | tf_op jit(solution)/shard_map/ppermute | solution.py:214
  22.0 10.4 %collective-permute-start.9 = (bf16[4,2,16,256]{3,2,1,0:T(8,128)(2,1)S(1)}, bf16[4,2,16,256]{3,2,1,0:T(8,128)(2,1)}, u32[]{:S(2)}, u32[]{:S(2)}) collective-permute-start(bf16[4,2,16,256]{3,2,1,0:T(8,128)(2,1)S(1)} %pad_maximum_fusion.refs_0_), channel_id=1, source_target_pairs={{64,0},{68,4},{72,8},{76,12},{80,16},{84,20},{88,24},{92,28},{96,3... | collective-permute-start | bytes 196616 | tf_op jit(solution)/shard_map/ppermute | solution.py:214
  23.5 9.6 %collective-permute-start.3 = (bf16[4,2,16,256]{3,2,1,0:T(8,128)(2,1)S(1)}, bf16[4,2,16,256]{3,2,1,0:T(8,128)(2,1)S(1)}, u32[]{:S(2)}, u32[]{:S(2)}) collective-permute-start(bf16[4,2,16,256]{3,2,1,0:T(8,128)(2,1)S(1)} %pad_maximum_fusion.refs_0_), channel_id=1, source_target_pairs={{4,0},{0,4},{12,8},{8,12},{20,16},{16,20},{28,24},{24,28},{36,32},... | collective-permute-start | bytes 196616 | tf_op jit(solution)/shard_map/ppermute | solution.py:214
  28.5 6.5 %collective-permute-start.15 = (bf16[4,2,16,256]{3,2,1,0:T(8,128)(2,1)S(1)}, bf16[4,2,16,256]{3,2,1,0:T(8,128)(2,1)}, u32[]{:S(2)}, u32[]{:S(2)}) collective-permute-start(bf16[4,2,16,256]{3,2,1,0:T(8,128)(2,1)S(1)} %pad_maximum_fusion.1.refs_2_), channel_id=1, source_target_pairs={{192,0},{196,4},{200,8},{204,12},{208,16},{212,20},{216,24},{220,2... | collective-permute-start | bytes 196616 | tf_op jit(solution)/shard_map/ppermute | solution.py:214
  28.6 6.6 %collective-permute-start.11 = (bf16[4,2,16,256]{3,2,1,0:T(8,128)(2,1)S(1)}, bf16[4,2,16,256]{3,2,1,0:T(8,128)(2,1)}, u32[]{:S(2)}, u32[]{:S(2)}) collective-permute-start(bf16[4,2,16,256]{3,2,1,0:T(8,128)(2,1)S(1)} %pad_maximum_fusion.1.refs_2_), channel_id=1, source_target_pairs={{64,0},{68,4},{72,8},{76,12},{80,16},{84,20},{88,24},{92,28},{96,3... | collective-permute-start | bytes 196616 | tf_op jit(solution)/shard_map/ppermute | solution.py:214
  31.2 5.0 %collective-permute-start.8 = (bf16[4,2,16,256]{3,2,1,0:T(8,128)(2,1)S(1)}, bf16[4,2,16,256]{3,2,1,0:T(8,128)(2,1)S(1)}, u32[]{:S(2)}, u32[]{:S(2)}) collective-permute-start(bf16[4,2,16,256]{3,2,1,0:T(8,128)(2,1)S(1)} %pad_maximum_fusion.1.refs_2_), channel_id=1, source_target_pairs={{4,0},{0,4},{12,8},{8,12},{20,16},{16,20},{28,24},{24,28},{36,32},... | collective-permute-start | bytes 196616 | tf_op jit(solution)/shard_map/ppermute | solution.py:214
  32.4 4.4 %collective-permute-start.19 = (bf16[4,2,16,256]{3,2,1,0:T(8,128)(2,1)S(1)}, bf16[4,2,16,256]{3,2,1,0:T(8,128)(2,1)S(1)}, u32[]{:S(2)}, u32[]{:S(2)}) collective-permute-start(bf16[4,2,16,256]{3,2,1,0:T(8,128)(2,1)S(1)} %collective-permute-done.18.refs_12_), channel_id=1, source_target_pairs={{4,0},{0,4},{12,8},{8,12},{20,16},{16,20},{28,24},{24,28},{36,32},... | collective-permute-start | bytes 196616 | tf_op jit(solution)/shard_map/ppermute | solution.py:214
  33.7 4.3 %collective-permute-start.13 = (bf16[4,2,16,256]{3,2,1,0:T(8,128)(2,1)}, bf16[4,2,16,256]{3,2,1,0:T(8,128)(2,1)}, u32[]{:S(2)}, u32[]{:S(2)}) collective-permute-start(bf16[4,2,16,256]{3,2,1,0:T(8,128)(2,1)} %collective-permute-done.9.refs_4_), channel_id=1, source_target_pairs={{64,0},{68,4},{72,8},{76,12},{80,16},{84,20},{88,24},{92,28},{96,3... | collective-permute-start | bytes 196616 | tf_op jit(solution)/shard_map/ppermute | solution.py:214
  35.0 4.6 %collective-permute-start.16 = (bf16[4,2,16,256]{3,2,1,0:T(8,128)(2,1)}, bf16[4,2,16,256]{3,2,1,0:T(8,128)(2,1)}, u32[]{:S(2)}, u32[]{:S(2)}) collective-permute-start(bf16[4,2,16,256]{3,2,1,0:T(8,128)(2,1)} %collective-permute-done.15.refs_14_), channel_id=1, source_target_pairs={{192,0},{196,4},{200,8},{204,12},{208,16},{212,20},{216,24},{220,2... | collective-permute-start | bytes 196616 | tf_op jit(solution)/shard_map/ppermute | solution.py:214
  35.2 11.9 %collective-permute-start.10 = (bf16[4,2,16,256]{3,2,1,0:T(8,128)(2,1)}, bf16[4,2,16,256]{3,2,1,0:T(8,128)(2,1)}, u32[]{:S(2)}, u32[]{:S(2)}) collective-permute-start(bf16[4,2,16,256]{3,2,1,0:T(8,128)(2,1)} %collective-permute-done.9.refs_4_), channel_id=1, source_target_pairs={{4,0},{0,4},{12,8},{8,12},{20,16},{16,20},{28,24},{24,28},{36,32},... | collective-permute-start | bytes 196616 | tf_op jit(solution)/shard_map/ppermute | solution.py:214
  36.9 10.2 %collective-permute-start.20 = (bf16[4,2,16,256]{3,2,1,0:T(8,128)(2,1)}, bf16[4,2,16,256]{3,2,1,0:T(8,128)(2,1)}, u32[]{:S(2)}, u32[]{:S(2)}) collective-permute-start(bf16[4,2,16,256]{3,2,1,0:T(8,128)(2,1)} %collective-permute-done.15.refs_14_), channel_id=1, source_target_pairs={{4,0},{0,4},{12,8},{8,12},{20,16},{16,20},{28,24},{24,28},{36,32},... | collective-permute-start | bytes 196616 | tf_op jit(solution)/shard_map/ppermute | solution.py:214
  37.5 9.6 %collective-permute-start.12 = (bf16[4,2,16,256]{3,2,1,0:T(8,128)(2,1)}, bf16[4,2,16,256]{3,2,1,0:T(8,128)(2,1)}, u32[]{:S(2)}, u32[]{:S(2)}) collective-permute-start(bf16[4,2,16,256]{3,2,1,0:T(8,128)(2,1)} %collective-permute-done.11.refs_6_), channel_id=1, source_target_pairs={{4,0},{0,4},{12,8},{8,12},{20,16},{16,20},{28,24},{24,28},{36,32},... | collective-permute-start | bytes 196616 | tf_op jit(solution)/shard_map/ppermute | solution.py:214
  38.0 9.1 %collective-permute-start.14 = (bf16[4,2,16,256]{3,2,1,0:T(8,128)(2,1)}, bf16[4,2,16,256]{3,2,1,0:T(8,128)(2,1)}, u32[]{:S(2)}, u32[]{:S(2)}) collective-permute-start(bf16[4,2,16,256]{3,2,1,0:T(8,128)(2,1)} %collective-permute-done.13.refs_8_), channel_id=1, source_target_pairs={{4,0},{0,4},{12,8},{8,12},{20,16},{16,20},{28,24},{24,28},{36,32},... | collective-permute-start | bytes 196616 | tf_op jit(solution)/shard_map/ppermute | solution.py:214
  39.7 7.5 %collective-permute-start.17 = (bf16[4,2,16,256]{3,2,1,0:T(8,128)(2,1)}, bf16[4,2,16,256]{3,2,1,0:T(8,128)(2,1)}, u32[]{:S(2)}, u32[]{:S(2)}) collective-permute-start(bf16[4,2,16,256]{3,2,1,0:T(8,128)(2,1)} %collective-permute-done.16.refs_10_), channel_id=1, source_target_pairs={{4,0},{0,4},{12,8},{8,12},{20,16},{16,20},{28,24},{24,28},{36,32},... | collective-permute-start | bytes 196616 | tf_op jit(solution)/shard_map/ppermute | solution.py:214
  57.7 5.7 %collective-permute-start.24 = (bf16[256,256]{1,0:T(8,128)(2,1)S(1)}, bf16[256,256]{1,0:T(8,128)(2,1)S(1)}, u32[]{:S(2)}, u32[]{:S(2)}) collective-permute-start(bf16[256,256]{1,0:T(8,128)(2,1)S(1)} %get-tuple-element.11), channel_id=1, source_target_pairs={{0,3},{1,0},{2,1},{3,2},{4,7},{5,4},{6,5},{7,6},{8,11},{9,8},{10,9... | collective-permute-start | bytes 393224 | tf_op jit(solution)/shard_map/ppermute | solution.py:218
  60.5 12.2 %collective-permute-start.21 = (bf16[256,256]{1,0:T(8,128)(2,1)S(1)}, bf16[256,256]{1,0:T(8,128)(2,1)S(1)}, u32[]{:S(2)}, u32[]{:S(2)}) collective-permute-start(bf16[256,256]{1,0:T(8,128)(2,1)S(1)} %get-tuple-element.12), channel_id=1, source_target_pairs={{0,1},{1,2},{2,3},{3,0},{4,5},{5,6},{6,7},{7,4},{8,9},{9,10},{10,1... | collective-permute-start | bytes 393224 | tf_op jit(solution)/shard_map/ppermute | solution.py:218
  68.7 12.2 %collective-permute-start.26 = (bf16[256,256]{1,0:T(8,128)(2,1)S(1)}, bf16[256,256]{1,0:T(8,128)(2,1)S(1)}, u32[]{:S(2)}, u32[]{:S(2)}) collective-permute-start(bf16[256,256]{1,0:T(8,128)(2,1)S(1)} %get-tuple-element.9), channel_id=1, source_target_pairs={{0,3},{1,0},{2,1},{3,2},{4,7},{5,4},{6,5},{7,6},{8,11},{9,8},{10,9... | collective-permute-start | bytes 393224 | tf_op jit(solution)/shard_map/ppermute | solution.py:218
  72.7 8.3 %collective-permute-start.25 = (bf16[256,256]{1,0:T(8,128)(2,1)S(1)}, bf16[256,256]{1,0:T(8,128)(2,1)S(1)}, u32[]{:S(2)}, u32[]{:S(2)}) collective-permute-start(bf16[256,256]{1,0:T(8,128)(2,1)S(1)} %get-tuple-element.10), channel_id=1, source_target_pairs={{0,1},{1,2},{2,3},{3,0},{4,5},{5,6},{6,7},{7,4},{8,9},{9,10},{10,1... | collective-permute-start | bytes 393224 | tf_op jit(solution)/shard_map/ppermute | solution.py:218
  78.0 4.9 %collective-permute-start.23 = (bf16[256,256]{1,0:T(8,128)(2,1)S(1)}, bf16[256,256]{1,0:T(8,128)(2,1)S(1)}, u32[]{:S(2)}, u32[]{:S(2)}) collective-permute-start(bf16[256,256]{1,0:T(8,128)(2,1)S(1)} %get-tuple-element.13), channel_id=1, source_target_pairs={{0,3},{1,0},{2,1},{3,2},{4,7},{5,4},{6,5},{7,6},{8,11},{9,8},{10,9... | collective-permute-start | bytes 393224 | tf_op jit(solution)/shard_map/ppermute | solution.py:218
  80.9 5.0 %collective-permute-start.22 = (bf16[256,256]{1,0:T(8,128)(2,1)S(1)}, bf16[256,256]{1,0:T(8,128)(2,1)S(1)}, u32[]{:S(2)}, u32[]{:S(2)}) collective-permute-start(bf16[256,256]{1,0:T(8,128)(2,1)S(1)} %get-tuple-element.14), channel_id=1, source_target_pairs={{0,1},{1,2},{2,3},{3,0},{4,5},{5,6},{6,7},{7,4},{8,9},{9,10},{10,1... | collective-permute-start | bytes 393224 | tf_op jit(solution)/shard_map/ppermute | solution.py:218
  (16 other events, 36.8 us)

commit v2 on v0

v2 whole, which is shorter than its diff:
```python
import functools

import jax
import jax.numpy as jnp
from jax import lax
from jax.experimental import pallas as pl
from jax.experimental.pallas import tpu as pltpu
from jax.sharding import PartitionSpec as P

SLOTS = 256
NX, NZ, NC, NY = 4, 8, 2, 4
ROWS = 16
CHUNK = NZ * NC * ROWS
BF, F32, I32 = jnp.bfloat16, jnp.float32, jnp.int32
VMEM = pl.BlockSpec(memory_space=pltpu.VMEM)
ANY = pl.BlockSpec(memory_space=pl.ANY)
SMALL = pltpu.CompilerParams(vmem_limit_bytes=8 << 20)
LARGE = pltpu.CompilerParams(vmem_limit_bytes=20 << 20)


def coords():
    w = lax.axis_index("wide")
    return w // (NZ * NC), (w // NC) % NZ, w % NC, lax.axis_index("depth")


def pick(row, index):
    lane = lax.broadcasted_iota(I32, row.shape, 1)
    return jnp.sum(jnp.where(lane == index, row, 0), axis=1, keepdims=True)


def pack_matrix(slot):
    row = lax.broadcasted_iota(I32, (SLOTS, slot.shape[1]), 0)
    return jnp.where(row == slot, 1.0, 0.0).astype(BF)


def column(row):
    return jnp.transpose(jnp.broadcast_to(row, (8, row.shape[1])))[:, :1]


def dot(left, right, on_left=1, on_right=0):
    return lax.dot_general(
        left, right, (((on_left,), (on_right,)), ((), ())), preferred_element_type=F32
    )


def compact_kernel(t_hbm, orb_hbm, pair_hbm, packed_ref, slot_ref, t_ref, orb_ref, pair_ref, sem):
    copies = [
        pltpu.make_async_copy(source, target, sem.at[i])
        for i, (source, target) in enumerate(((orb_hbm, orb_ref), (pair_hbm, pair_ref), (t_hbm, t_ref)))
    ]
    for copy in copies:
        copy.start()
    for copy in copies:
        copy.wait()
    x, z, core, y = coords()
    w = (x * NZ + z) * NC + core
    rows, c_count, n = t_ref.shape
    orb = orb_ref[...]
    member = jnp.where(lax.broadcasted_iota(I32, (8, n), 0) == orb, 1.0, 0.0)
    upto = jnp.where(
        lax.broadcasted_iota(I32, (128, 128), 0) <= lax.broadcasted_iota(I32, (128, 128), 1), 1.0, 0.0
    ).astype(BF)
    before = jnp.zeros((8, 1), F32)
    counts = []
    for start in range(0, n, 128):
        size = min(128, n - start)
        part = member[:, start:start + size]
        counts.append(dot(part.astype(BF), upto[:size, :size]) + before)
        before = before + jnp.sum(part, axis=1, keepdims=True)
    count = jnp.concatenate(counts, axis=1)
    slot = jnp.sum(member * count, axis=0, keepdims=True).astype(I32) - 1
    slot_ref[...] = slot
    onehot = pack_matrix(slot)
    pair = pair_ref[...]
    lane = lax.broadcasted_iota(I32, (rows, pair.shape[1]), 1)
    row = lax.broadcasted_iota(I32, (rows, pair.shape[1]), 0)
    pair_col = jnp.sum(jnp.where(lane == row + w * rows, pair, 0), axis=1, keepdims=True)
    amps = t_ref[...]
    for c in range(c_count):
        label = pick(orb, y * c_count + c)
        kept = jnp.where(orb == (pair_col ^ label), amps[:, c, :].astype(F32), 0.0).astype(BF)
        packed_ref[c] = dot(kept, onehot, 1, 1).astype(BF)


def compact(amplitudes, orb, pair):
    rows, c_count, n = amplitudes.shape
    return pl.pallas_call(
        compact_kernel,
        out_shape=(
            jax.ShapeDtypeStruct((c_count, rows, SLOTS), BF),
            jax.ShapeDtypeStruct((1, n), I32),
        ),
        in_specs=[pl.BlockSpec(memory_space=pltpu.HBM)] * 3,
        out_specs=(VMEM, VMEM),
        scratch_shapes=[
            pltpu.VMEM(amplitudes.shape, BF),
            pltpu.VMEM(orb.shape, I32),
            pltpu.VMEM(pair.shape, I32),
            pltpu.SemaphoreType.DMA((3,)),
        ],
        compiler_params=SMALL,
        name="compact",
    )(amplitudes, orb, pair)


def tables_kernel(orb_ref, slot_ref, _, pack_ref, unpack_ref, orb_col_ref):
    n = orb_ref.shape[1]
    slot = slot_ref[...]
    pack_ref[...] = pack_matrix(slot)
    lane = lax.broadcasted_iota(I32, (n, SLOTS), 1)
    unpack_ref[...] = jnp.where(lane == column(slot), 1.0, 0.0).astype(BF)
    orb_col_ref[...] = jnp.broadcast_to(column(orb_ref[...]), (n, 128))


def tables(orb, slot, after):
    n = orb.shape[1]
    return pl.pallas_call(
        tables_kernel,
        out_shape=(
            jax.ShapeDtypeStruct((SLOTS, n), BF),
            jax.ShapeDtypeStruct((n, SLOTS), BF),
            jax.ShapeDtypeStruct((n, 128), I32),
        ),
        in_specs=[VMEM] * 2 + [ANY],
        out_specs=(VMEM,) * 3,
        compiler_params=SMALL,
        name="tables",
    )(orb, slot, after)


def pair_of(pair_ref, dest):
    total = jnp.zeros((1, CHUNK), I32)
    for k in range(NY):
        total = total + jnp.where(dest == k, pair_ref[:, CHUNK * k:CHUNK * (k + 1)], 0)
    return total


def keep_matrix(orb_col_ref, label, pair_row):
    wanted = pair_row ^ label
    orb_col = orb_col_ref[...]
    return jnp.concatenate(
        [orb_col == wanted[:, at:at + 128] for at in range(0, CHUNK, 128)], axis=1
    )


def partial_kernel(offsets, *refs):
    held, v_ref = refs[:4], refs[4]
    orb_ref, pair_ref, pack_ref, unpack_ref = refs[5:9]
    out_refs, (rows_ref,) = refs[9:-1], refs[-1:]
    x, z, core, y = coords()
    w = (x * NZ + z) * NC + core
    orb = orb_ref[...]
    for i, off in enumerate(offsets):
        dest = lax.rem(y + off, NY)
        rel = x ^ dest
        for other in range(NC):
            near, late = held[2 * other:2 * other + 2]
            source = core ^ other
            first = 1 + 2 * source
            is_late = (rel != 0) & (rel != first)
            index = jnp.where(rel == first, 1, jnp.where(rel == 2, 1, 0))
            for j in range(NZ):
                zz = z ^ (7 * (j & 1)) ^ (2 * (j >> 1 & 1)) ^ (j >> 2 & 1)
                at = pl.multiple_of((zz * NC + source) * ROWS, ROWS)
                for c in range(2):
                    value = jnp.where(is_late, late[index, j, c], near[index, j, c])
                    rows_ref[i, c, pl.ds(at, ROWS), :] = value
        pair_col = jnp.broadcast_to(column(pair_of(pair_ref, dest)), (CHUNK, orb.shape[1]))
        spread = []
        for c in range(2):
            full = dot(rows_ref[i, c], pack_ref[...])
            keep = orb == (pair_col ^ pick(orb, y * 2 + c))
            spread.append(jnp.where(keep, full, 0.0).astype(BF))
        for a in range(2):
            total = dot(spread[0], v_ref[a, 0]) + dot(spread[1], v_ref[a, 1])
            keep = orb == (pair_col ^ pick(orb, w * 2 + a))
            kept = jnp.where(keep, total, 0.0).astype(BF)
            packed = dot(kept, unpack_ref[...]).astype(BF)
            out_refs[i][a] = packed


def partial(held, v, orb, pair, table, offsets):
    n = orb.shape[1]
    out_shape = [jax.ShapeDtypeStruct((2, CHUNK, SLOTS), BF)] * len(offsets)
    return pl.pallas_call(
        functools.partial(partial_kernel, offsets),
        out_shape=out_shape,
        in_specs=[VMEM] * 9,
        out_specs=[VMEM] * len(out_shape),
        scratch_shapes=[pltpu.VMEM((len(offsets), 2, CHUNK, SLOTS), BF)],
        compiler_params=LARGE,
        cost_estimate=pl.CostEstimate(
            flops=8 * CHUNK * n * n * len(offsets), bytes_accessed=8 * n * n, transcendentals=0
        ),
        name="partial",
    )(*held, v, orb, pair, *table[:2])


def join_kernel(up_ref, down_ref, far_ref, up_out, down_out):
    upward = lax.axis_index("wide") % NC == 0

    @pl.when(upward)
    def _():
        up_out[...] = (up_ref[...].astype(F32) + far_ref[...].astype(F32)).astype(BF)
        down_out[...] = down_ref[...]

    @pl.when(jnp.logical_not(upward))
    def _():
        up_out[...] = up_ref[...]
        down_out[...] = (down_ref[...].astype(F32) + far_ref[...].astype(F32)).astype(BF)


def join(up, down, far):
    return pl.pallas_call(
        join_kernel,
        out_shape=[jax.ShapeDtypeStruct(up.shape, BF)] * 2,
        in_specs=[VMEM] * 3,
        out_specs=[VMEM] * 2,
        compiler_params=SMALL,
        name="join",
    )(up, down, far)


def finish_kernel(own_ref, up_ref, down_ref, orb_ref, pair_ref, unpack_ref, orb_col_ref, out_ref):
    x, z, core, y = coords()
    w = (x * NZ + z) * NC + core
    pair_row = pair_of(pair_ref, y)
    orb = orb_ref[...]
    for a in range(2):
        total = own_ref[a].astype(F32) + up_ref[a].astype(F32) + down_ref[a].astype(F32)
        full = dot(unpack_ref[...], total.astype(BF), 1, 1)
        keep = keep_matrix(orb_col_ref, pick(orb, w * 2 + a), pair_row)
        out_ref[a] = jnp.where(keep, full, 0.0).astype(BF)


def finish(own, up, down, orb, pair, table):
    n = orb.shape[1]
    return pl.pallas_call(
        finish_kernel,
        out_shape=jax.ShapeDtypeStruct((2, n, CHUNK), BF),
        in_specs=[VMEM] * 7,
        out_specs=VMEM,
        compiler_params=SMALL,
        name="finish",
    )(own, up, down, orb, pair, *table[1:])


def swap(value, partner):
    index = lambda x, z, c: (x * NZ + z) * NC + c
    return lax.ppermute(
        value,
        "wide",
        [
            (index(x, z, c), index(*partner(x, z, c)))
            for x in range(NX) for z in range(NZ) for c in range(NC)
        ],
    )


def to_depth(value, dy_of_core):
    width = NX * NZ * NC
    return lax.ppermute(
        value,
        ("wide", "depth"),
        [(w * NY + y, w * NY + (y + dy_of_core[w % NC]) % NY) for w in range(width) for y in range(NY)],
    )


def tie_kernel(*refs):
    pass


def tie(values, *others):
    count = len(values)
    return pl.pallas_call(
        tie_kernel,
        out_shape=[jax.ShapeDtypeStruct(value.shape, value.dtype) for value in values],
        in_specs=[ANY] * (count + len(others)),
        out_specs=[ANY] * count,
        input_output_aliases={i: i for i in range(count)},
        compiler_params=SMALL,
        name="tie",
    )(*values, *others)


def gather(block, beside):
    other = lambda x, z, c: (x, z, 1 - c)
    block = block[None]
    for bit in (7, 2, 1):
        block = jnp.concatenate([block, swap(block, lambda x, z, c: (x, z ^ bit, c))])
    near = jnp.stack([block, swap(block, lambda x, z, c: (x ^ (1 + 2 * c), z, c))])
    late = swap(near, lambda x, z, c: (x ^ (3 - 2 * c), z, c))
    near_other = swap(near, other)
    (late,) = tie([late], *beside)
    return near, late, near_other, swap(late, other)


def local(amplitudes, integrals, orbital_irrep, pair_irrep):
    n = integrals.shape[1]
    orb = orbital_irrep.reshape(1, n)
    pair = pair_irrep.reshape(1, pair_irrep.shape[0])
    v = jnp.transpose(integrals, (2, 0, 1, 3))
    packed, slot = compact(amplitudes, orb, pair)
    table = tables(orb, slot, v)
    held = gather(packed, table)
    call = functools.partial(partial, held, v, orb, pair, table)
    (far,) = call((2,))
    far = to_depth(far, (1, -1))
    up, down = call((1, 3))
    up, down = join(up, down, far)
    up, down = to_depth(up, (1, 1)), to_depth(down, (-1, -1))
    (own,) = call((0,))
    out = finish(own, up, down, orb, pair, table)
    return jnp.transpose(out, (2, 0, 1))


def solution(mesh):
    placed = (P("wide", "depth", None), P("depth", None, "wide", None), P(), P())
    return jax.shard_map(
        local, mesh=mesh, in_specs=placed, out_specs=P("depth", "wide", None), check_vma=False
    )
```

time: 175 us -> 63.7 us (0.36)
  waiting for transfers between devices: 92.7 us -> 10.5 us
  local copies, waits for them, and re-layouts: 33.3 us -> 8.2 us
  starting transfers between devices: 0.04 us -> 25.1 us
  other arithmetic: 19.9 us -> 0.76 us
  Pallas kernels: 0 us -> 18.7 us
  matrix products: 14.3 us -> 0 us
  between operations: 13.4 us -> 0.11 us
    all_gather x1 -> x0, waiting for transfers between devices: 47.1 us -> none  [local(): piece = lax.all_gather(amplitudes, 'wide', axis=0, tiled=True)]
    reduce_scatter x1 -> x0, waiting for transfers between devices: 44.9 us -> none  [local(): lax.psum_scatter(partial_sum.astype(jnp.bfloat16), 'depth', scatter_dimen...]
    ppermute x0 -> x10, starting transfers between devices: none -> 25.1 us  [the longest x7 19.4 us: swap(): lax.ppermute(value, 'wide', [(index(x, z, c), index(*partner(x, z, c))) f...]
    reshape x1 -> x0, local copies, waits for them, and re-layouts: 20.5 us -> none  [local(): jnp.where(allowed, integrals, jnp.zeros((), jnp.bfloat16))]
    pallas_call x0 -> x8, Pallas kernels: none -> 18.7 us  [the longest x3 15.8 us: partial(): pl.pallas_call(functools.partial(partial_kernel, offsets), out_shape=out_...]
    select_n x1 -> x0, other arithmetic: 16.9 us -> none  [local(): jnp.where(allowed, integrals, jnp.zeros((), jnp.bfloat16))]
    dot_general x1 -> x0, matrix products: 14.3 us -> none  [local(): jnp.dot(piece.reshape(piece.shape[0], c_count * orbitals), masked, prefer...]
    all_gather x1 -> x0, local copies, waits for them, and re-layouts: 11.2 us -> none  [local(): piece = lax.all_gather(amplitudes, 'wide', axis=0, tiled=True)]
  transfers between devices with their start and end apart: 2 -> 10, of which waited for: 2 -> 7; matrix products, arithmetic and copies ran while one was open for 23% -> 9% of each run, Pallas kernels for 0% -> 19%
where the time goes in v2:
time: 63.7 us; the launch traced here: 63.4 us
  starting transfers between devices  25.1 us (39%)
  Pallas kernels  18.7 us (29%)
  waiting for transfers between devices  10.5 us (16%)
  local copies, waits for them, and re-layouts  8.2 us (13%)
  other arithmetic  0.76 us (1%)
    ppermute x7, starting transfers between devices, swap(): lax.ppermute(value, 'wide', [(index(x, z, c), index(*partner(x, z, c))) f...  19.4 us
    pallas_call x3, Pallas kernels, partial(): pl.pallas_call(functools.partial(partial_kernel, offsets), out_shape=out_...  15.8 us
    ppermute x7, waiting for transfers between devices, swap(): lax.ppermute(value, 'wide', [(index(x, z, c), index(*partner(x, z, c))) f...  8.56 us
    unnamed x11, local copies, waits for them, and re-layouts  8.2 us
    ppermute x3, starting transfers between devices, to_depth(): lax.ppermute(value, ('wide', 'depth'), [(w * NY + y, w * NY + (y + dy_of_...  5.73 us
    ppermute x3, waiting for transfers between devices, to_depth(): lax.ppermute(value, ('wide', 'depth'), [(w * NY + y, w * NY + (y + dy_of_...  1.93 us
    pallas_call x1, Pallas kernels, finish(): pl.pallas_call(finish_kernel, out_shape=jax.ShapeDtypeStruct((2, n, CHUNK...  1.46 us
  transfers between devices with their start and end apart: 10, of which 7 were waited for; matrix products, arithmetic and copies ran while one was open for 9% of the time, Pallas kernels for 19%

profile of v2, /device:TPU:1, one launch (start us, length us, event | category | flops | bytes accessed | tf_op | source)
XLA Modules:
  0.0 63.4 jit_solution(9941159665620384462)
XLA Ops:
  0.0 0.7 %copy-done = s32[1000]{0:T(1024)S(1)} copy-done((s32[1000]{0:T(1024)S(1)}, s32[1000]{0:T(1024)}, u32[]{:S(2)}) %copy-start) | copy-done | bytes 4024
  0.7 0.7 %copy-done.2 = s32[1024]{0:T(1024)S(1)} copy-done((s32[1024]{0:T(1024)S(1)}, s32[1024]{0:T(1024)}, u32[]{:S(2)}) %copy-start.2) | copy-done | bytes 4120
  1.4 0.8 %copy-done.4 = bf16[16,2,1000]{2,1,0:T(2,128)(2,1)S(1)} copy-done((bf16[16,2,1000]{2,1,0:T(2,128)(2,1)S(1)}, bf16[16,2,1000]{2,1,0:T(2,128)(2,1)}, u32[]{:S(2)}) %copy-start.4) | copy-done | bytes 64024
  2.2 0.6 %compact.1 = (bf16[2,16,256]{2,1,0:T(8,128)(2,1)S(1)}, s32[1,1000]{1,0:T(1,128)S(1)}) custom-call(bf16[16,2,1000]{2,1,0:T(2,128)(2,1)S(1)} %copy-done.4, s32[1,1000]{1,0:T(1,128)S(1)} %bitcast.18, s32[1,1024]{1,0:T(1,128)S(1)} %bitcast.24), custom_call_target="tpu_custom_call" | custom-call | tf_op jit(solution)/shard_map/compact/pallas_call | solution.py:87
  2.9 6.5 %collective-permute-start = (bf16[1,2,16,256]{3,2,1,0:T(8,128)(2,1)S(1)}, bf16[1,2,16,256]{3,2,1,0:T(8,128)(2,1)S(1)}, u32[]{:S(2)}, u32[]{:S(2)}) collective-permute-start(bf16[1,2,16,256]{3,2,1,0:T(8,128)(2,1)S(1)} %bitcast.14), channel_id=1, source_target_pairs={{0,56},{4,60},{8,48},{12,52},{16,40},{20,44},{24,32},{28,36},{32,2... | collective-permute-start | bytes 49160 | tf_op jit(solution)/shard_map/ppermute | solution.py:250
  9.4 1.1 %collective-permute-done = bf16[1,2,16,256]{3,2,1,0:T(8,128)(2,1)S(1)} collective-permute-done((bf16[1,2,16,256]{3,2,1,0:T(8,128)(2,1)S(1)}, bf16[1,2,16,256]{3,2,1,0:T(8,128)(2,1)S(1)}, u32[]{:S(2)}, u32[]{:S(2)}) %collective-permute-start) | collective-permute-done | bytes 16416 | tf_op jit(solution)/shard_map/ppermute | solution.py:250
  10.5 2.1 %collective-permute-start.1 = (bf16[2,2,16,256]{3,2,1,0:T(8,128)(2,1)S(1)}, bf16[2,2,16,256]{3,2,1,0:T(8,128)(2,1)S(1)}, u32[]{:S(2)}, u32[]{:S(2)}) collective-permute-start(bf16[2,2,16,256]{3,2,1,0:T(8,128)(2,1)S(1)} %pad_maximum_fusion.3), channel_id=1, source_target_pairs={{0,16},{4,20},{8,24},{12,28},{16,0},{20,4},{24,8},{28,12},{32,48},... | collective-permute-start | bytes 98312 | tf_op jit(solution)/shard_map/ppermute | solution.py:250
  12.6 1.6 %collective-permute-done.1 = bf16[2,2,16,256]{3,2,1,0:T(8,128)(2,1)S(1)} collective-permute-done((bf16[2,2,16,256]{3,2,1,0:T(8,128)(2,1)S(1)}, bf16[2,2,16,256]{3,2,1,0:T(8,128)(2,1)S(1)}, u32[]{:S(2)}, u32[]{:S(2)}) %collective-permute-start.1) | collective-permute-done | bytes 32800 | tf_op jit(solution)/shard_map/ppermute | solution.py:250
  14.2 1.7 %collective-permute-start.2 = (bf16[4,2,16,256]{3,2,1,0:T(8,128)(2,1)S(1)}, bf16[4,2,16,256]{3,2,1,0:T(8,128)(2,1)S(1)}, u32[]{:S(2)}, u32[]{:S(2)}) collective-permute-start(bf16[4,2,16,256]{3,2,1,0:T(8,128)(2,1)S(1)} %pad_maximum_fusion.2), channel_id=1, source_target_pairs={{0,8},{4,12},{8,0},{12,4},{16,24},{20,28},{24,16},{28,20},{32,40},... | collective-permute-start | bytes 196616 | tf_op jit(solution)/shard_map/ppermute | solution.py:250
  15.9 1.7 %collective-permute-done.2 = bf16[4,2,16,256]{3,2,1,0:T(8,128)(2,1)S(1)} collective-permute-done((bf16[4,2,16,256]{3,2,1,0:T(8,128)(2,1)S(1)}, bf16[4,2,16,256]{3,2,1,0:T(8,128)(2,1)S(1)}, u32[]{:S(2)}, u32[]{:S(2)}) %collective-permute-start.2) | collective-permute-done | bytes 65568 | tf_op jit(solution)/shard_map/ppermute | solution.py:250
  17.6 2.6 %collective-permute-start.3 = (bf16[8,2,16,256]{3,2,1,0:T(8,128)(2,1)S(1)}, bf16[8,2,16,256]{3,2,1,0:T(8,128)(2,1)S(1)}, u32[]{:S(2)}, u32[]{:S(2)}) collective-permute-start(bf16[8,2,16,256]{3,2,1,0:T(8,128)(2,1)S(1)} %get-tuple-element.24), channel_id=1, source_target_pairs={{0,64},{4,196},{8,72},{12,204},{16,80},{20,212},{24,88},{28,220},{... | collective-permute-start | bytes 393224 | tf_op jit(solution)/shard_map/ppermute | solution.py:250
  20.1 2.5 %collective-permute-done.3 = bf16[8,2,16,256]{3,2,1,0:T(8,128)(2,1)S(1)} collective-permute-done((bf16[8,2,16,256]{3,2,1,0:T(8,128)(2,1)S(1)}, bf16[8,2,16,256]{3,2,1,0:T(8,128)(2,1)S(1)}, u32[]{:S(2)}, u32[]{:S(2)}) %collective-permute-start.3) | collective-permute-done | bytes 131104 | tf_op jit(solution)/shard_map/ppermute | solution.py:250
  22.7 0.7 %pad_maximum_fusion.refs_0_ = bf16[2,8,2,16,256]{4,3,2,1,0:T(8,128)(2,1)} fusion(bf16[1,8,2,16,256]{4,3,2,1,0:T(8,128)(2,1)S(1)} %bitcast.29, bf16[1,8,2,16,256]{4,3,2,1,0:T(8,128)(2,1)S(1)} %get-tuple-element.23), kind=kLoop, calls=%fused_computation.1 | loop fusion | flops 131072 | bytes 524288 | tf_op jit(solution)/shard_map/stack | solution.py:291
  23.4 6.0 %copy.8 = bf16[2,1000,2,1000]{3,1,0,2:T(8,128)(2,1)S(1)} copy(bf16[2,1000,2,1000]{3,2,1,0:T(2,128)(2,1)} %param.5) | data formatting | bytes 16000000 | tf_op args[1]
  29.4 0.7 %tables.1 = (bf16[256,1000]{1,0:T(8,128)(2,1)S(1)}, bf16[1000,256]{1,0:T(8,128)(2,1)S(1)}, s32[1000,128]{1,0:T(8,128)S(1)}) custom-call(s32[1,1000]{1,0:T(1,128)S(1)} %bitcast.19, s32[1,1000]{1,0:T(1,128)S(1)} %get-tuple-element.15.slot_ref, bf16[2,2,1000,1000]{3,2,1,0:T(8,128)(2,1)S(1)} %bitcast.10), custom_call_target="tpu_custom_call" | custom-call | tf_op jit(solution)/shard_map/tables/pallas_call | solution.py:117
  30.2 6.4 %collective-permute-start.5 = (bf16[2,8,2,16,256]{4,3,2,1,0:T(8,128)(2,1)}, bf16[2,8,2,16,256]{4,3,2,1,0:T(8,128)(2,1)S(1)}, u32[]{:S(2)}, u32[]{:S(2)}) collective-permute-start(bf16[2,8,2,16,256]{4,3,2,1,0:T(8,128)(2,1)} %pad_maximum_fusion.refs_0_), channel_id=1, source_target_pairs={{0,4},{4,0},{8,12},{12,8},{16,20},{20,16},{24,28},{28,24},{32,36},... | collective-permute-start | bytes 786440 | tf_op jit(solution)/shard_map/ppermute | solution.py:250
  36.7 1.3 %collective-permute-done.5.refs_2_ = bf16[2,8,2,16,256]{4,3,2,1,0:T(8,128)(2,1)S(1)} collective-permute-done((bf16[2,8,2,16,256]{4,3,2,1,0:T(8,128)(2,1)}, bf16[2,8,2,16,256]{4,3,2,1,0:T(8,128)(2,1)S(1)}, u32[]{:S(2)}, u32[]{:S(2)}) %collective-permute-start.5) | collective-permute-done | bytes 262176 | tf_op jit(solution)/shard_map/ppermute | solution.py:250
  38.4 4.3 %partial.5 = bf16[2,256,256]{2,1,0:T(8,128)(2,1)S(1)} custom-call(bf16[2,8,2,16,256]{4,3,2,1,0:T(8,128)(2,1)} %pad_maximum_fusion.refs_0_, bf16[2,8,2,16,256]{4,3,2,1,0:T(8,128)(2,1)} %tie.1.refs_1_, bf16[2,8,2,16,256]{4,3,2,1,0:T(8,128)(2,1)S(1)} %collective-permute-done.5.refs_2_, bf16[2,8,2,16,256]{4,3,2,1,0:T(8,128)(2,1)S(1)} %collective-permute-done.6.refs_3_, ...), custom_call_target="tpu_custom_call" | custom-call | flops 2048000000 | bytes 8000000 | tf_op jit(solution)/shard_map/partial/pallas_call | solution.py:185
  42.7 3.0 %collective-permute-start.7 = (bf16[2,256,256]{2,1,0:T(8,128)(2,1)S(1)}, bf16[2,256,256]{2,1,0:T(8,128)(2,1)S(1)}, u32[]{:S(2)}, u32[]{:S(2)}) collective-permute-start(bf16[2,256,256]{2,1,0:T(8,128)(2,1)S(1)} %partial.5), channel_id=1, source_target_pairs={{0,1},{1,2},{2,3},{3,0},{4,7},{5,4},{6,5},{7,6},{8,9},{9,10},{10,1... | collective-permute-start | bytes 786440 | tf_op jit(solution)/shard_map/ppermute | solution.py:262
  45.7 7.2 %partial.4 = (bf16[2,256,256]{2,1,0:T(8,128)(2,1)S(1)}, bf16[2,256,256]{2,1,0:T(8,128)(2,1)S(1)}) custom-call(bf16[2,8,2,16,256]{4,3,2,1,0:T(8,128)(2,1)} %pad_maximum_fusion.refs_0_, bf16[2,8,2,16,256]{4,3,2,1,0:T(8,128)(2,1)} %tie.1.refs_1_, bf16[2,8,2,16,256]{4,3,2,1,0:T(8,128)(2,1)S(1)} %collective-permute-done.5.refs_2_, ...), custom_call_target="tpu_custom_call" | custom-call | flops 4096000000 | bytes 8000000 | tf_op jit(solution)/shard_map/partial/pallas_call | solution.py:185
  53.1 2.7 %collective-permute-start.9 = (bf16[2,256,256]{2,1,0:T(8,128)(2,1)S(1)}, bf16[2,256,256]{2,1,0:T(8,128)(2,1)S(1)}, u32[]{:S(2)}, u32[]{:S(2)}) collective-permute-start(bf16[2,256,256]{2,1,0:T(8,128)(2,1)S(1)} %get-tuple-element.22), channel_id=1, source_target_pairs={{0,3},{1,0},{2,1},{3,2},{4,7},{5,4},{6,5},{7,6},{8,11},{9,8},{10,9... | collective-permute-start | bytes 786440 | tf_op jit(solution)/shard_map/ppermute | solution.py:262
  55.7 4.3 %partial.3.own_ref = bf16[2,256,256]{2,1,0:T(8,128)(2,1)S(1)} custom-call(bf16[2,8,2,16,256]{4,3,2,1,0:T(8,128)(2,1)} %pad_maximum_fusion.refs_0_, bf16[2,8,2,16,256]{4,3,2,1,0:T(8,128)(2,1)} %tie.1.refs_1_, bf16[2,8,2,16,256]{4,3,2,1,0:T(8,128)(2,1)S(1)} %collective-permute-done.5.refs_2_, bf16[2,8,2,16,256]{4,3,2,1,0:T(8,128)(2,1)S(1)} %collective-permute-done.6.refs_3_, ...), custom_call_target="tpu_custom_call" | custom-call | flops 2048000000 | bytes 8000000 | tf_op jit(solution)/shard_map/partial/pallas_call | solution.py:185
  60.0 1.9 %collective-permute-done.8.up_ref = bf16[2,256,256]{2,1,0:T(8,128)(2,1)S(1)} collective-permute-done((bf16[2,256,256]{2,1,0:T(8,128)(2,1)S(1)}, bf16[2,256,256]{2,1,0:T(8,128)(2,1)S(1)}, u32[]{:S(2)}, u32[]{:S(2)}) %collective-permute-start.8) | collective-permute-done | bytes 262176 | tf_op jit(solution)/shard_map/ppermute | solution.py:262
  62.0 1.5 %finish.1 = bf16[2,1000,256]{2,1,0:T(8,128)(2,1)} custom-call(bf16[2,256,256]{2,1,0:T(8,128)(2,1)S(1)} %partial.3.own_ref, bf16[2,256,256]{2,1,0:T(8,128)(2,1)S(1)} %collective-permute-done.8.up_ref, bf16[2,256,256]{2,1,0:T(8,128)(2,1)S(1)} %collective-permute-done.9.down_ref, s32[1,1000]{1,0:T(1,128)S(1)} %bitcast.23, s32[1,1024]{1,0:T(1,128)S(1)} %bitcast.28, ...), custom_call_target="tpu_custom_call" | custom-call | tf_op jit(solution)/shard_map/finish/pallas_call | solution.py:238
  (19 shorter events, 0.7 us)
Async XLA Ops:
  0.0 0.7 %copy-start = (s32[1000]{0:T(1024)S(1)}, s32[1000]{0:T(1024)}, u32[]{:S(2)}) copy-start(s32[1000]{0:T(1024)} %param.6) | copy-start | bytes 12004
  0.7 0.7 %copy-start.2 = (s32[1024]{0:T(1024)S(1)}, s32[1024]{0:T(1024)}, u32[]{:S(2)}) copy-start(s32[1024]{0:T(1024)} %param.7) | copy-start | bytes 12292
  1.4 0.8 %copy-start.4 = (bf16[16,2,1000]{2,1,0:T(2,128)(2,1)S(1)}, bf16[16,2,1000]{2,1,0:T(2,128)(2,1)}, u32[]{:S(2)}) copy-start(bf16[16,2,1000]{2,1,0:T(2,128)(2,1)} %t_hbm.1) | copy-start | bytes 192004
  2.9 7.6 %collective-permute-start = (bf16[1,2,16,256]{3,2,1,0:T(8,128)(2,1)S(1)}, bf16[1,2,16,256]{3,2,1,0:T(8,128)(2,1)S(1)}, u32[]{:S(2)}, u32[]{:S(2)}) collective-permute-start(bf16[1,2,16,256]{3,2,1,0:T(8,128)(2,1)S(1)} %bitcast.14), channel_id=1, source_target_pairs={{0,56},{4,60},{8,48},{12,52},{16,40},{20,44},{24,32},{28,36},{32,2... | collective-permute-start | bytes 49160 | tf_op jit(solution)/shard_map/ppermute | solution.py:250
  10.5 3.7 %collective-permute-start.1 = (bf16[2,2,16,256]{3,2,1,0:T(8,128)(2,1)S(1)}, bf16[2,2,16,256]{3,2,1,0:T(8,128)(2,1)S(1)}, u32[]{:S(2)}, u32[]{:S(2)}) collective-permute-start(bf16[2,2,16,256]{3,2,1,0:T(8,128)(2,1)S(1)} %pad_maximum_fusion.3), channel_id=1, source_target_pairs={{0,16},{4,20},{8,24},{12,28},{16,0},{20,4},{24,8},{28,12},{32,48},... | collective-permute-start | bytes 98312 | tf_op jit(solution)/shard_map/ppermute | solution.py:250
  14.2 3.4 %collective-permute-start.2 = (bf16[4,2,16,256]{3,2,1,0:T(8,128)(2,1)S(1)}, bf16[4,2,16,256]{3,2,1,0:T(8,128)(2,1)S(1)}, u32[]{:S(2)}, u32[]{:S(2)}) collective-permute-start(bf16[4,2,16,256]{3,2,1,0:T(8,128)(2,1)S(1)} %pad_maximum_fusion.2), channel_id=1, source_target_pairs={{0,8},{4,12},{8,0},{12,4},{16,24},{20,28},{24,16},{28,20},{32,40},... | collective-permute-start | bytes 196616 | tf_op jit(solution)/shard_map/ppermute | solution.py:250
  17.6 5.1 %collective-permute-start.3 = (bf16[8,2,16,256]{3,2,1,0:T(8,128)(2,1)S(1)}, bf16[8,2,16,256]{3,2,1,0:T(8,128)(2,1)S(1)}, u32[]{:S(2)}, u32[]{:S(2)}) collective-permute-start(bf16[8,2,16,256]{3,2,1,0:T(8,128)(2,1)S(1)} %get-tuple-element.24), channel_id=1, source_target_pairs={{0,64},{4,196},{8,72},{12,204},{16,80},{20,212},{24,88},{28,220},{... | collective-permute-start | bytes 393224 | tf_op jit(solution)/shard_map/ppermute | solution.py:250
  23.4 6.0 %copy-start.1 = (s32[1000]{0:T(1024)S(1)}, s32[1000]{0:T(1024)}, u32[]{:S(2)}) copy-start(s32[1000]{0:T(1024)} %param.6) | copy-start | bytes 12004
  23.4 13.2 %collective-permute-start.4 = (bf16[2,8,2,16,256]{4,3,2,1,0:T(8,128)(2,1)}, bf16[2,8,2,16,256]{4,3,2,1,0:T(8,128)(2,1)}, u32[]{:S(2)}, u32[]{:S(2)}) collective-permute-start(bf16[2,8,2,16,256]{4,3,2,1,0:T(8,128)(2,1)} %pad_maximum_fusion.refs_0_), channel_id=1, source_target_pairs={{0,192},{4,68},{8,200},{12,76},{16,208},{20,84},{24,216},{28,92},{... | collective-permute-start | bytes 786440 | tf_op jit(solution)/shard_map/ppermute | solution.py:250
  29.4 9.0 %copy-start.3 = (s32[1024]{0:T(1024)S(1)}, s32[1024]{0:T(1024)}, u32[]{:S(2)}) copy-start(s32[1024]{0:T(1024)} %param.7) | copy-start | bytes 12292
  30.2 7.8 %collective-permute-start.5 = (bf16[2,8,2,16,256]{4,3,2,1,0:T(8,128)(2,1)}, bf16[2,8,2,16,256]{4,3,2,1,0:T(8,128)(2,1)S(1)}, u32[]{:S(2)}, u32[]{:S(2)}) collective-permute-start(bf16[2,8,2,16,256]{4,3,2,1,0:T(8,128)(2,1)} %pad_maximum_fusion.refs_0_), channel_id=1, source_target_pairs={{0,4},{4,0},{8,12},{12,8},{16,20},{20,16},{24,28},{28,24},{32,36},... | collective-permute-start | bytes 786440 | tf_op jit(solution)/shard_map/ppermute | solution.py:250
  36.6 1.7 %collective-permute-start.6 = (bf16[2,8,2,16,256]{4,3,2,1,0:T(8,128)(2,1)}, bf16[2,8,2,16,256]{4,3,2,1,0:T(8,128)(2,1)S(1)}, u32[]{:S(2)}, u32[]{:S(2)}) collective-permute-start(bf16[2,8,2,16,256]{4,3,2,1,0:T(8,128)(2,1)} %tie.1.refs_1_), channel_id=1, source_target_pairs={{0,4},{4,0},{8,12},{12,8},{16,20},{20,16},{24,28},{28,24},{32,36},... | collective-permute-start | bytes 786440 | tf_op jit(solution)/shard_map/ppermute | solution.py:250
  42.7 10.2 %collective-permute-start.7 = (bf16[2,256,256]{2,1,0:T(8,128)(2,1)S(1)}, bf16[2,256,256]{2,1,0:T(8,128)(2,1)S(1)}, u32[]{:S(2)}, u32[]{:S(2)}) collective-permute-start(bf16[2,256,256]{2,1,0:T(8,128)(2,1)S(1)} %partial.5), channel_id=1, source_target_pairs={{0,1},{1,2},{2,3},{3,0},{4,7},{5,4},{6,5},{7,6},{8,9},{9,10},{10,1... | collective-permute-start | bytes 786440 | tf_op jit(solution)/shard_map/ppermute | solution.py:262
  53.0 9.0 %collective-permute-start.8 = (bf16[2,256,256]{2,1,0:T(8,128)(2,1)S(1)}, bf16[2,256,256]{2,1,0:T(8,128)(2,1)S(1)}, u32[]{:S(2)}, u32[]{:S(2)}) collective-permute-start(bf16[2,256,256]{2,1,0:T(8,128)(2,1)S(1)} %get-tuple-element.21), channel_id=1, source_target_pairs={{0,1},{1,2},{2,3},{3,0},{4,5},{5,6},{6,7},{7,4},{8,9},{9,10},{10,1... | collective-permute-start | bytes 786440 | tf_op jit(solution)/shard_map/ppermute | solution.py:262
  53.1 8.9 %collective-permute-start.9 = (bf16[2,256,256]{2,1,0:T(8,128)(2,1)S(1)}, bf16[2,256,256]{2,1,0:T(8,128)(2,1)S(1)}, u32[]{:S(2)}, u32[]{:S(2)}) collective-permute-start(bf16[2,256,256]{2,1,0:T(8,128)(2,1)S(1)} %get-tuple-element.22), channel_id=1, source_target_pairs={{0,3},{1,0},{2,1},{3,2},{4,7},{5,4},{6,5},{7,6},{8,11},{9,8},{10,9... | collective-permute-start | bytes 786440 | tf_op jit(solution)/shard_map/ppermute | solution.py:262

commit v3 on v2

v3 whole, which is shorter than its diff:
```python
import functools

import jax
import jax.numpy as jnp
from jax import lax
from jax.experimental import pallas as pl
from jax.experimental.pallas import tpu as pltpu
from jax.sharding import PartitionSpec as P

SLOTS = 256
NX, NZ, NC, NY = 4, 8, 2, 4
BLOCK, HALF = 128, 512
ROWS = 16
CHUNK = NZ * NC * ROWS
PAIRS = NX * CHUNK
BF, F32, I32 = jnp.bfloat16, jnp.float32, jnp.int32
VMEM = pl.BlockSpec(memory_space=pltpu.VMEM)
ANY = pl.BlockSpec(memory_space=pl.ANY)
SMALL = pltpu.CompilerParams(vmem_limit_bytes=8 << 20)
HELD = pltpu.CompilerParams(vmem_limit_bytes=50 << 20)
LARGE = pltpu.CompilerParams(vmem_limit_bytes=20 << 20)


def coords():
    w = lax.axis_index("wide")
    return w // (NZ * NC), (w // NC) % NZ, w % NC, lax.axis_index("depth")


def pick(row, index):
    lane = lax.broadcasted_iota(I32, row.shape, 1)
    return jnp.sum(jnp.where(lane == index, row, 0), axis=1, keepdims=True)


def pack_matrix(slot):
    row = lax.broadcasted_iota(I32, (SLOTS, slot.shape[1]), 0)
    return jnp.where(row == slot, 1.0, 0.0).astype(BF)


def orb_of(labels_ref):
    return labels_ref[:, PAIRS:]


def column(row):
    return jnp.transpose(jnp.broadcast_to(row, (8, row.shape[1])))[:, :1]


def dot(left, right, on_left=1, on_right=0):
    return lax.dot_general(
        left, right, (((on_left,), (on_right,)), ((), ())), preferred_element_type=F32
    )


def compact_kernel(t_ref, labels_ref, packed_ref, slot_ref):
    x, z, core, y = coords()
    w = (x * NZ + z) * NC + core
    rows, c_count, n = t_ref.shape
    orb = orb_of(labels_ref)
    member = jnp.where(lax.broadcasted_iota(I32, (8, n), 0) == orb, 1.0, 0.0)
    upto = jnp.where(
        lax.broadcasted_iota(I32, (128, 128), 0) <= lax.broadcasted_iota(I32, (128, 128), 1), 1.0, 0.0
    ).astype(BF)
    before = jnp.zeros((8, 1), F32)
    counts = []
    for start in range(0, n, 128):
        size = min(128, n - start)
        part = member[:, start:start + size]
        counts.append(dot(part.astype(BF), upto[:size, :size]) + before)
        before = before + jnp.sum(part, axis=1, keepdims=True)
    count = jnp.concatenate(counts, axis=1)
    slot = jnp.sum(member * count, axis=0, keepdims=True).astype(I32) - 1
    slot_ref[...] = slot
    onehot = pack_matrix(slot)
    pair = labels_ref[:, :PAIRS]
    lane = lax.broadcasted_iota(I32, (rows, pair.shape[1]), 1)
    row = lax.broadcasted_iota(I32, (rows, pair.shape[1]), 0)
    pair_col = jnp.sum(jnp.where(lane == row + w * rows, pair, 0), axis=1, keepdims=True)
    amps = t_ref[...]
    for c in range(c_count):
        label = pick(orb, y * c_count + c)
        kept = jnp.where(orb == (pair_col ^ label), amps[:, c, :].astype(F32), 0.0).astype(BF)
        packed_ref[c] = dot(kept, onehot, 1, 1).astype(BF)


def compact(amplitudes, labels):
    rows, c_count, n = amplitudes.shape
    return pl.pallas_call(
        compact_kernel,
        out_shape=(
            jax.ShapeDtypeStruct((c_count, rows, SLOTS), BF),
            jax.ShapeDtypeStruct((1, n), I32),
        ),
        in_specs=[VMEM] * 2,
        out_specs=(VMEM, VMEM),
        compiler_params=SMALL,
        name="compact",
    )(amplitudes, labels)


def unweave_kernel(c, start, v_hbm, out_ref, held, sem):
    _, rows, n = out_ref.shape
    sizes = [min(BLOCK, rows - at) for at in range(0, rows, BLOCK)]
    copies = [
        pltpu.make_async_copy(
            v_hbm.at[c, pl.ds(start + k * BLOCK, size)], held.at[pl.ds(k * BLOCK, size)], sem.at[k]
        )
        for k, size in enumerate(sizes)
    ]
    for copy in copies:
        copy.start()
    for k, (size, copy) in enumerate(zip(sizes, copies)):
        to = lax.broadcasted_iota(I32, (2 * size, 2 * size), 0)
        of = lax.broadcasted_iota(I32, (2 * size, 2 * size), 1)
        order = jnp.where(of == jnp.where(to < size, 2 * to, 2 * (to - size) + 1), 1.0, 0.0).astype(BF)
        copy.wait()
        at = k * BLOCK
        both = dot(order, held[at:at + size].reshape(2 * size, n)).astype(BF)
        out_ref[0, at:at + size] = both[:size]
        out_ref[1, at:at + size] = both[size:]


def unweave(v, c, start, rows):
    _, _, a_count, n = v.shape
    return pl.pallas_call(
        functools.partial(unweave_kernel, c, start),
        out_shape=jax.ShapeDtypeStruct((a_count, rows, n), BF),
        in_specs=[ANY],
        out_specs=VMEM,
        scratch_shapes=[
            pltpu.VMEM((rows, a_count, n), BF),
            pltpu.SemaphoreType.DMA((-(-rows // BLOCK),)),
        ],
        compiler_params=HELD,
        cost_estimate=pl.CostEstimate(
            flops=8 * BLOCK * rows * n, bytes_accessed=8 * rows * n, transcendentals=0
        ),
        name="unweave",
    )(v)


def tables_kernel(labels_ref, slot_ref, pack_ref, unpack_ref, orb_col_ref):
    n = slot_ref.shape[1]
    slot = slot_ref[...]
    pack_ref[...] = pack_matrix(slot)
    lane = lax.broadcasted_iota(I32, (n, SLOTS), 1)
    unpack_ref[...] = jnp.where(lane == column(slot), 1.0, 0.0).astype(BF)
    orb_col_ref[...] = jnp.broadcast_to(column(orb_of(labels_ref)), (n, 128))


def tables(labels, slot):
    n = slot.shape[1]
    return pl.pallas_call(
        tables_kernel,
        out_shape=(
            jax.ShapeDtypeStruct((SLOTS, n), BF),
            jax.ShapeDtypeStruct((n, SLOTS), BF),
            jax.ShapeDtypeStruct((n, 128), I32),
        ),
        in_specs=[VMEM] * 2,
        out_specs=(VMEM,) * 3,
        compiler_params=SMALL,
        name="tables",
    )(labels, slot)


def pair_of(labels_ref, dest):
    total = jnp.zeros((1, CHUNK), I32)
    for k in range(NY):
        total = total + jnp.where(dest == k, labels_ref[:, CHUNK * k:CHUNK * (k + 1)], 0)
    return total


def keep_matrix(orb_col_ref, label, pair_row):
    wanted = pair_row ^ label
    orb_col = orb_col_ref[...]
    return jnp.concatenate(
        [orb_col == wanted[:, at:at + 128] for at in range(0, CHUNK, 128)], axis=1
    )


def partial_kernel(turn, *refs):
    held, v_refs = refs[:4], refs[4:8]
    labels_ref, pack_ref, unpack_ref, out_ref, rows_ref = refs[8:]
    x, z, core, y = coords()
    w = (x * NZ + z) * NC + core
    orb = orb_of(labels_ref)
    dest = y ^ jnp.where(core == 0, *turn)
    rel = x ^ dest
    index = jnp.where(rel == 3, 2, jnp.where(rel == 1, 1, 0))
    for other in range(NC):
        near, last = held[2 * other:2 * other + 2]
        source = core ^ other
        for j in range(NZ):
            zz = z ^ (7 * (j & 1)) ^ (2 * (j >> 1 & 1)) ^ (j >> 2)
            at = pl.multiple_of((zz * NC + source) * ROWS, ROWS)
            for c in range(2):
                rows_ref[c, pl.ds(at, ROWS), :] = jnp.where(rel == 2, last[j, c], near[index, j, c])
    pair_col = jnp.broadcast_to(column(pair_of(labels_ref, dest)), (CHUNK, orb.shape[1]))
    spread = []
    for c in range(2):
        full = dot(rows_ref[c], pack_ref[...])
        keep = orb == (pair_col ^ pick(orb, y * 2 + c))
        kept = jnp.where(keep, full, 0.0).astype(BF)
        spread += [kept[:, :HALF], kept[:, HALF:]]
    for a in range(2):
        total = sum(dot(left, v_ref[a]) for left, v_ref in zip(spread, v_refs))
        keep = orb == (pair_col ^ pick(orb, w * 2 + a))
        kept = jnp.where(keep, total, 0.0).astype(BF)
        out_ref[a] = dot(kept, unpack_ref[...]).astype(BF)


def partial(held, v, labels, table, turn):
    n = table[0].shape[1]
    return pl.pallas_call(
        functools.partial(partial_kernel, turn),
        out_shape=jax.ShapeDtypeStruct((2, CHUNK, SLOTS), BF),
        in_specs=[VMEM] * 11,
        out_specs=VMEM,
        scratch_shapes=[pltpu.VMEM((2, CHUNK, SLOTS), BF)],
        compiler_params=LARGE,
        cost_estimate=pl.CostEstimate(flops=8 * CHUNK * n * n, bytes_accessed=8 * n * n, transcendentals=0),
        name="partial",
    )(*held, *v, labels, *table[:2])


def add_kernel(left_ref, right_ref, out_ref):
    out_ref[...] = (left_ref[...].astype(F32) + right_ref[...].astype(F32)).astype(BF)


def add(left, right):
    return pl.pallas_call(
        add_kernel,
        out_shape=jax.ShapeDtypeStruct(left.shape, BF),
        in_specs=[VMEM] * 2,
        out_specs=VMEM,
        compiler_params=SMALL,
        name="add",
    )(left, right)


def finish_kernel(*refs):
    part_refs, (labels_ref, unpack_ref, orb_col_ref, out_ref, held, sem) = refs[:3], refs[3:]
    x, z, core, y = coords()
    w = (x * NZ + z) * NC + core
    pair_row = pair_of(labels_ref, y)
    orb = orb_of(labels_ref)
    n = orb.shape[1]
    cuts = [(a, pl.ds(at, min(HALF, n - at))) for a in range(2) for at in (0, HALF)]
    copies = [
        pltpu.make_async_copy(held.at[a, cut], out_ref.at[a, cut], sem.at[k]) for k, (a, cut) in enumerate(cuts)
    ]
    for a in range(2):
        total = sum(part_ref[a].astype(F32) for part_ref in part_refs)
        total = total.astype(BF)
        keep = keep_matrix(orb_col_ref, pick(orb, w * 2 + a), pair_row)
        for k, (of, cut) in enumerate(cuts):
            if of == a:
                full = dot(unpack_ref[cut, :], total, 1, 1)
                held[a, cut, :] = jnp.where(keep[cut.start:cut.start + cut.size], full, 0.0).astype(BF)
                copies[k].start()
    for copy in copies:
        copy.wait()


def finish(parts, labels, table):
    shape = (2, table[0].shape[1], CHUNK)
    return pl.pallas_call(
        finish_kernel,
        out_shape=jax.ShapeDtypeStruct(shape, BF),
        in_specs=[VMEM] * 6,
        out_specs=ANY,
        scratch_shapes=[pltpu.VMEM(shape, BF), pltpu.SemaphoreType.DMA((4,))],
        compiler_params=SMALL,
        name="finish",
    )(*parts, labels, *table[1:])


def swap(value, partner):
    index = lambda x, z, c: (x * NZ + z) * NC + c
    return lax.ppermute(
        value,
        "wide",
        [
            (index(x, z, c), index(*partner(x, z, c)))
            for x in range(NX) for z in range(NZ) for c in range(NC)
        ],
    )


def to_depth(value, turn):
    return lax.ppermute(
        value,
        ("wide", "depth"),
        [(w * NY + y, w * NY + (y ^ turn[w % NC])) for w in range(NX * NZ * NC) for y in range(NY)],
    )


def tie_kernel(*refs):
    pass


def tie(values, *others):
    count = len(values)
    return pl.pallas_call(
        tie_kernel,
        out_shape=[jax.ShapeDtypeStruct(value.shape, value.dtype) for value in values],
        in_specs=[ANY] * (count + len(others)),
        out_specs=[ANY] * count,
        input_output_aliases={i: i for i in range(count)},
        compiler_params=SMALL,
        name="tie",
    )(*values, *others)


def gather(block, beside):
    other = lambda x, z, c: (x, z, 1 - c)
    along_z = lambda value, bits: swap(value, lambda x, z, c: (x, z ^ bits, c))
    along_x = lambda value, bits: swap(value, lambda x, z, c: (x ^ bits, z, c))
    block = block[None]
    for k, bits in enumerate((7, 2, 1)):
        block = jnp.concatenate([block, *tie([along_z(block, bits)], *beside[k])])
    sent = swap(block, other)
    got = tie([along_x(block, bits) for bits in (1, 3)], *beside[3])
    last = along_x(got[0], 3)
    got_other = [swap(value, other) for value in got]
    (last,) = tie([last], *got_other, *beside[4])
    return jnp.stack([block, *got]), last, jnp.stack([sent, *got_other]), swap(last, other)


def local(amplitudes, integrals, orbital_irrep, pair_irrep):
    n = integrals.shape[1]
    labels = jnp.concatenate([pair_irrep, orbital_irrep]).reshape(1, PAIRS + n)
    v = [unweave(integrals, c, at, min(HALF, n - at)) for c in range(2) for at in (0, HALF)]
    packed, slot = compact(amplitudes, labels)
    table = tables(labels, slot)
    held = gather(packed, (table, [v[0]], [v[1]], [v[2]], [v[3]]))
    one, two = (3, 1), (1, 3)
    call = functools.partial(partial, held, v, labels, table)
    far = to_depth(call((2, 2)), one)
    direct = to_depth(call(one), one)
    summed = to_depth(add(call(two), far), two)
    out = finish([call((0, 0)), direct, summed], labels, table)
    return jnp.transpose(out, (2, 0, 1))


def solution(mesh):
    placed = (P("wide", "depth", None), P("depth", None, "wide", None), P(), P())
    return jax.shard_map(
        local, mesh=mesh, in_specs=placed, out_specs=P("depth", "wide", None), check_vma=False
    )
```

time: 63.7 us -> 57.9 us (0.909)
  local copies, waits for them, and re-layouts: 8.2 us -> 0.84 us
  Pallas kernels: 18.7 us -> 25.2 us
  waiting for transfers between devices: 10.5 us -> 4.77 us
    unnamed x11 -> x2, local copies, waits for them, and re-layouts: 8.2 us -> 0.84 us
    pallas_call x5 -> x10, Pallas kernels: 17.3 us -> 24 us  [the longest x4 13.3 us: partial(): pl.pallas_call(functools.partial(partial_kernel, turn), out_shape=jax.Sha...]
    ppermute x7 -> x10, waiting for transfers between devices: 8.56 us -> 2.95 us  [swap(): lax.ppermute(value, 'wide', [(index(x, z, c), index(*partner(x, z, c))) f...]
    ppermute x7 -> x10, starting transfers between devices: 19.4 us -> 21 us  [swap(): lax.ppermute(value, 'wide', [(index(x, z, c), index(*partner(x, z, c))) f...]
    ppermute x3, starting transfers between devices: 5.73 us -> 4.67 us  [to_depth(): lax.ppermute(value, ('wide', 'depth'), [(w * NY + y, w * NY + (y ^ turn[w...]
    concatenate x2 -> x3, other arithmetic: 0.01 us -> 0.72 us  [the longest x1 0.71 us: local(): labels = jnp.concatenate([pair_irrep, orbital_irrep]).reshape(1, PAIRS + n)]
  transfers between devices with their start and end apart: 10 -> 13, of which waited for: 7 -> 5; matrix products, arithmetic and copies ran while one was open for 9% -> 0% of each run, Pallas kernels for 19% -> 35%
where the time goes in v3:
time: 57.9 us; the launch traced here: 57.7 us
  starting transfers between devices  25.6 us (44%)
  Pallas kernels  25.2 us (44%)
  waiting for transfers between devices  4.77 us (8%)
  other arithmetic  0.84 us (1%)
  local copies, waits for them, and re-layouts  0.84 us (1%)
    ppermute x10, starting transfers between devices, swap(): lax.ppermute(value, 'wide', [(index(x, z, c), index(*partner(x, z, c))) f...  21 us
    pallas_call x4, Pallas kernels, partial(): pl.pallas_call(functools.partial(partial_kernel, turn), out_shape=jax.Sha...  13.3 us
    pallas_call x4, Pallas kernels, unweave(): pl.pallas_call(functools.partial(unweave_kernel, c, start), out_shape=jax...  9.29 us
    ppermute x3, starting transfers between devices, to_depth(): lax.ppermute(value, ('wide', 'depth'), [(w * NY + y, w * NY + (y ^ turn[w...  4.67 us
    ppermute x10, waiting for transfers between devices, swap(): lax.ppermute(value, 'wide', [(index(x, z, c), index(*partner(x, z, c))) f...  2.95 us
    ppermute x3, waiting for transfers between devices, to_depth(): lax.ppermute(value, ('wide', 'depth'), [(w * NY + y, w * NY + (y ^ turn[w...  1.82 us
    pallas_call x1, Pallas kernels, finish(): pl.pallas_call(finish_kernel, out_shape=jax.ShapeDtypeStruct(shape, BF),...  1.34 us
  transfers between devices with their start and end apart: 13, of which 5 were waited for; matrix products, arithmetic and copies ran while one was open for 0% of the time, Pallas kernels for 35%

profile of v3, /device:TPU:1, one launch (start us, length us, event | category | flops | bytes accessed | tf_op | source)
XLA Modules:
  0.0 57.7 jit_solution(9632418866168174680)
XLA Ops:
  0.7 0.8 %copy-done = bf16[16,2,1000]{2,1,0:T(2,128)(2,1)S(1)} copy-done((bf16[16,2,1000]{2,1,0:T(2,128)(2,1)S(1)}, bf16[16,2,1000]{2,1,0:T(2,128)(2,1)}, u32[]{:S(2)}) %copy-start) | copy-done | bytes 64024
  2.1 6.4 %collective-permute-start = (bf16[1,2,16,256]{3,2,1,0:T(8,128)(2,1)S(1)}, bf16[1,2,16,256]{3,2,1,0:T(8,128)(2,1)S(1)}, u32[]{:S(2)}, u32[]{:S(2)}) collective-permute-start(bf16[1,2,16,256]{3,2,1,0:T(8,128)(2,1)S(1)} %bitcast.21), channel_id=1, source_target_pairs={{0,56},{4,60},{8,48},{12,52},{16,40},{20,44},{24,32},{28,36},{32,2... | collective-permute-start | bytes 49160 | tf_op jit(solution)/shard_map/ppermute | solution.py:279
  9.6 2.1 %collective-permute-start.1 = (bf16[2,2,16,256]{3,2,1,0:T(8,128)(2,1)S(1)}, bf16[2,2,16,256]{3,2,1,0:T(8,128)(2,1)S(1)}, u32[]{:S(2)}, u32[]{:S(2)}) collective-permute-start(bf16[2,2,16,256]{3,2,1,0:T(8,128)(2,1)S(1)} %pad_maximum_fusion.4), channel_id=1, source_target_pairs={{0,16},{4,20},{8,24},{12,28},{16,0},{20,4},{24,8},{28,12},{32,48},... | collective-permute-start | bytes 98312 | tf_op jit(solution)/shard_map/ppermute | solution.py:279
  11.7 2.3 %unweave.4.refs_1_.refs_4_ = bf16[2,512,1000]{2,1,0:T(8,128)(2,1)S(1)} custom-call(bf16[2,1000,2,1000]{3,2,1,0:T(2,128)(2,1)} %v_hbm.7), custom_call_target="tpu_custom_call" | custom-call | flops 524288000 | bytes 4096000 | tf_op jit(solution)/shard_map/unweave/pallas_call | solution.py:123
  14.1 0.9 %collective-permute-start.2 = (bf16[4,2,16,256]{3,2,1,0:T(8,128)(2,1)S(1)}, bf16[4,2,16,256]{3,2,1,0:T(8,128)(2,1)S(1)}, u32[]{:S(2)}, u32[]{:S(2)}) collective-permute-start(bf16[4,2,16,256]{3,2,1,0:T(8,128)(2,1)S(1)} %pad_maximum_fusion.3), channel_id=1, source_target_pairs={{0,8},{4,12},{8,0},{12,4},{16,24},{20,28},{24,16},{28,20},{32,40},... | collective-permute-start | bytes 196616 | tf_op jit(solution)/shard_map/ppermute | solution.py:279
  15.0 2.3 %unweave.5.refs_1_.refs_5_ = bf16[2,488,1000]{2,1,0:T(8,128)(2,1)S(1)} custom-call(bf16[2,1000,2,1000]{3,2,1,0:T(2,128)(2,1)} %v_hbm.7), custom_call_target="tpu_custom_call" | custom-call | flops 499712000 | bytes 3904000 | tf_op jit(solution)/shard_map/unweave/pallas_call | solution.py:123
  17.4 1.3 %collective-permute-start.3 = (bf16[8,2,16,256]{3,2,1,0:T(8,128)(2,1)S(1)}, bf16[8,2,16,256]{3,2,1,0:T(8,128)(2,1)S(1)}, u32[]{:S(2)}, u32[]{:S(2)}) collective-permute-start(bf16[8,2,16,256]{3,2,1,0:T(8,128)(2,1)S(1)} %get-tuple-element.20), channel_id=1, source_target_pairs={{0,64},{4,68},{8,72},{12,76},{16,80},{20,84},{24,88},{28,92},{32,9... | collective-permute-start | bytes 393224 | tf_op jit(solution)/shard_map/ppermute | solution.py:279
  18.7 1.8 %collective-permute-start.4 = (bf16[8,2,16,256]{3,2,1,0:T(8,128)(2,1)S(1)}, bf16[8,2,16,256]{3,2,1,0:T(8,128)(2,1)S(1)}, u32[]{:S(2)}, u32[]{:S(2)}) collective-permute-start(bf16[8,2,16,256]{3,2,1,0:T(8,128)(2,1)S(1)} %get-tuple-element.20), channel_id=1, source_target_pairs={{0,192},{4,196},{8,200},{12,204},{16,208},{20,212},{24,216},{28,22... | collective-permute-start | bytes 393224 | tf_op jit(solution)/shard_map/ppermute | solution.py:279
  20.5 2.3 %unweave.6.refs_2_.refs_6_ = bf16[2,512,1000]{2,1,0:T(8,128)(2,1)S(1)} custom-call(bf16[2,1000,2,1000]{3,2,1,0:T(2,128)(2,1)} %v_hbm.7), custom_call_target="tpu_custom_call" | custom-call | flops 524288000 | bytes 4096000 | tf_op jit(solution)/shard_map/unweave/pallas_call | solution.py:123
  22.9 0.8 %collective-permute-done.4.refs_1_ = bf16[8,2,16,256]{3,2,1,0:T(8,128)(2,1)S(1)} collective-permute-done((bf16[8,2,16,256]{3,2,1,0:T(8,128)(2,1)S(1)}, bf16[8,2,16,256]{3,2,1,0:T(8,128)(2,1)S(1)}, u32[]{:S(2)}, u32[]{:S(2)}) %collective-permute-start.4) | collective-permute-done | bytes 131104 | tf_op jit(solution)/shard_map/ppermute | solution.py:279
  23.7 4.4 %collective-permute-start.6 = (bf16[8,2,16,256]{3,2,1,0:T(8,128)(2,1)S(1)}, bf16[8,2,16,256]{3,2,1,0:T(8,128)(2,1)S(1)}, u32[]{:S(2)}, u32[]{:S(2)}) collective-permute-start(bf16[8,2,16,256]{3,2,1,0:T(8,128)(2,1)S(1)} %get-tuple-element.17), channel_id=1, source_target_pairs={{0,4},{4,0},{8,12},{12,8},{16,20},{20,16},{24,28},{28,24},{32,36},... | collective-permute-start | bytes 393224 | tf_op jit(solution)/shard_map/ppermute | solution.py:279
  28.1 1.8 %collective-permute-start.5 = (bf16[8,2,16,256]{3,2,1,0:T(8,128)(2,1)S(1)}, bf16[8,2,16,256]{3,2,1,0:T(8,128)(2,1)S(1)}, u32[]{:S(2)}, u32[]{:S(2)}) collective-permute-start(bf16[8,2,16,256]{3,2,1,0:T(8,128)(2,1)S(1)} %get-tuple-element.17), channel_id=1, source_target_pairs={{0,192},{4,196},{8,200},{12,204},{16,208},{20,212},{24,216},{28,22... | collective-permute-start | bytes 393224 | tf_op jit(solution)/shard_map/ppermute | solution.py:279
  30.8 2.3 %unweave.7.refs_3_.refs_7_ = bf16[2,488,1000]{2,1,0:T(8,128)(2,1)S(1)} custom-call(bf16[2,1000,2,1000]{3,2,1,0:T(2,128)(2,1)} %v_hbm.7), custom_call_target="tpu_custom_call" | custom-call | flops 499712000 | bytes 3904000 | tf_op jit(solution)/shard_map/unweave/pallas_call | solution.py:123
  33.1 0.8 %collective-permute-done.5.refs_0_ = bf16[8,2,16,256]{3,2,1,0:T(8,128)(2,1)S(1)} collective-permute-done((bf16[8,2,16,256]{3,2,1,0:T(8,128)(2,1)S(1)}, bf16[8,2,16,256]{3,2,1,0:T(8,128)(2,1)S(1)}, u32[]{:S(2)}, u32[]{:S(2)}) %collective-permute-start.5) | collective-permute-done | bytes 131104 | tf_op jit(solution)/shard_map/ppermute | solution.py:279
  33.9 1.4 %collective-permute-start.9 = (bf16[8,2,16,256]{3,2,1,0:T(8,128)(2,1)S(1)}, bf16[8,2,16,256]{3,2,1,0:T(8,128)(2,1)S(1)}, u32[]{:S(2)}, u32[]{:S(2)}) collective-permute-start(bf16[8,2,16,256]{3,2,1,0:T(8,128)(2,1)S(1)} %tie.9.refs_1_), channel_id=1, source_target_pairs={{0,4},{4,0},{8,12},{12,8},{16,20},{20,16},{24,28},{28,24},{32,36},... | collective-permute-start | bytes 393224 | tf_op jit(solution)/shard_map/ppermute | solution.py:279
  35.4 0.9 %collective-permute-done.9.refs_3_ = bf16[8,2,16,256]{3,2,1,0:T(8,128)(2,1)S(1)} collective-permute-done((bf16[8,2,16,256]{3,2,1,0:T(8,128)(2,1)S(1)}, bf16[8,2,16,256]{3,2,1,0:T(8,128)(2,1)S(1)}, u32[]{:S(2)}, u32[]{:S(2)}) %collective-permute-start.9) | collective-permute-done | bytes 131104 | tf_op jit(solution)/shard_map/ppermute | solution.py:279
  36.3 3.3 %partial.7 = bf16[2,256,256]{2,1,0:T(8,128)(2,1)S(1)} custom-call(bf16[3,8,2,16,256]{4,3,2,1,0:T(8,128)(2,1)S(1)} %pad_maximum_fusion.refs_0_, bf16[8,2,16,256]{3,2,1,0:T(8,128)(2,1)S(1)} %tie.9.refs_1_, bf16[3,8,2,16,256]{4,3,2,1,0:T(8,128)(2,1)S(1)} %pad_maximum_fusion.1.refs_2_, bf16[8,2,16,256]{3,2,1,0:T(8,128)(2,1)S(1)} %collective-permute-done.9.refs_3_, ...), custom_call_target="tpu_custom_call" | custom-call | flops 2048000000 | bytes 8000000 | tf_op jit(solution)/shard_map/partial/pallas_call | solution.py:213
  39.6 1.4 %collective-permute-start.11 = (bf16[2,256,256]{2,1,0:T(8,128)(2,1)S(1)}, bf16[2,256,256]{2,1,0:T(8,128)(2,1)S(1)}, u32[]{:S(2)}, u32[]{:S(2)}) collective-permute-start(bf16[2,256,256]{2,1,0:T(8,128)(2,1)S(1)} %partial.7), channel_id=1, source_target_pairs={{0,3},{1,2},{2,1},{3,0},{4,5},{5,4},{6,7},{7,6},{8,11},{9,10},{10,... | collective-permute-start | bytes 786440 | tf_op jit(solution)/shard_map/ppermute | solution.py:290
  41.0 3.3 %partial.5 = bf16[2,256,256]{2,1,0:T(8,128)(2,1)S(1)} custom-call(bf16[3,8,2,16,256]{4,3,2,1,0:T(8,128)(2,1)S(1)} %pad_maximum_fusion.refs_0_, bf16[8,2,16,256]{3,2,1,0:T(8,128)(2,1)S(1)} %tie.9.refs_1_, bf16[3,8,2,16,256]{4,3,2,1,0:T(8,128)(2,1)S(1)} %pad_maximum_fusion.1.refs_2_, bf16[8,2,16,256]{3,2,1,0:T(8,128)(2,1)S(1)} %collective-permute-done.9.refs_3_, ...), custom_call_target="tpu_custom_call" | custom-call | flops 2048000000 | bytes 8000000 | tf_op jit(solution)/shard_map/partial/pallas_call | solution.py:213
  44.6 3.3 %partial.6.left_ref = bf16[2,256,256]{2,1,0:T(8,128)(2,1)S(1)} custom-call(bf16[3,8,2,16,256]{4,3,2,1,0:T(8,128)(2,1)S(1)} %pad_maximum_fusion.refs_0_, bf16[8,2,16,256]{3,2,1,0:T(8,128)(2,1)S(1)} %tie.9.refs_1_, bf16[3,8,2,16,256]{4,3,2,1,0:T(8,128)(2,1)S(1)} %pad_maximum_fusion.1.refs_2_, bf16[8,2,16,256]{3,2,1,0:T(8,128)(2,1)S(1)} %collective-permute-done.9.refs_3_, ...), custom_call_target="tpu_custom_call" | custom-call | flops 2048000000 | bytes 8000000 | tf_op jit(solution)/shard_map/partial/pallas_call | solution.py:213
  48.0 3.0 %collective-permute-start.12 = (bf16[2,256,256]{2,1,0:T(8,128)(2,1)S(1)}, bf16[2,256,256]{2,1,0:T(8,128)(2,1)S(1)}, u32[]{:S(2)}, u32[]{:S(2)}) collective-permute-start(bf16[2,256,256]{2,1,0:T(8,128)(2,1)S(1)} %add.3), channel_id=1, source_target_pairs={{0,1},{1,0},{2,3},{3,2},{4,7},{5,6},{6,5},{7,4},{8,9},{9,8},{10,11... | collective-permute-start | bytes 786440 | tf_op jit(solution)/shard_map/ppermute | solution.py:290
  51.0 3.3 %partial.4.refs_0_ = bf16[2,256,256]{2,1,0:T(8,128)(2,1)S(1)} custom-call(bf16[3,8,2,16,256]{4,3,2,1,0:T(8,128)(2,1)S(1)} %pad_maximum_fusion.refs_0_, bf16[8,2,16,256]{3,2,1,0:T(8,128)(2,1)S(1)} %tie.9.refs_1_, bf16[3,8,2,16,256]{4,3,2,1,0:T(8,128)(2,1)S(1)} %pad_maximum_fusion.1.refs_2_, bf16[8,2,16,256]{3,2,1,0:T(8,128)(2,1)S(1)} %collective-permute-done.9.refs_3_, ...), custom_call_target="tpu_custom_call" | custom-call | flops 2048000000 | bytes 8000000 | tf_op jit(solution)/shard_map/partial/pallas_call | solution.py:213
  54.3 1.8 %collective-permute-done.12.refs_2_ = bf16[2,256,256]{2,1,0:T(8,128)(2,1)S(1)} collective-permute-done((bf16[2,256,256]{2,1,0:T(8,128)(2,1)S(1)}, bf16[2,256,256]{2,1,0:T(8,128)(2,1)S(1)}, u32[]{:S(2)}, u32[]{:S(2)}) %collective-permute-start.12) | collective-permute-done | bytes 262176 | tf_op jit(solution)/shard_map/ppermute | solution.py:290
  56.2 1.3 %finish.1 = bf16[2,1000,256]{2,1,0:T(8,128)(2,1)} custom-call(bf16[2,256,256]{2,1,0:T(8,128)(2,1)S(1)} %partial.4.refs_0_, bf16[2,256,256]{2,1,0:T(8,128)(2,1)S(1)} %collective-permute-done.10.refs_1_, bf16[2,256,256]{2,1,0:T(8,128)(2,1)S(1)} %collective-permute-done.12.refs_2_, s32[1,2024]{1,0:T(1,128)S(1)} %bitcast.20, ...), custom_call_target="tpu_custom_call" | custom-call | tf_op jit(solution)/shard_map/finish/pallas_call | solution.py:266
  (27 shorter events, 3.6 us)
Async XLA Ops:
  0.7 0.8 %copy-start = (bf16[16,2,1000]{2,1,0:T(2,128)(2,1)S(1)}, bf16[16,2,1000]{2,1,0:T(2,128)(2,1)}, u32[]{:S(2)}) copy-start(bf16[16,2,1000]{2,1,0:T(2,128)(2,1)} %t_ref.1) | copy-start | bytes 192004
  2.1 7.6 %collective-permute-start = (bf16[1,2,16,256]{3,2,1,0:T(8,128)(2,1)S(1)}, bf16[1,2,16,256]{3,2,1,0:T(8,128)(2,1)S(1)}, u32[]{:S(2)}, u32[]{:S(2)}) collective-permute-start(bf16[1,2,16,256]{3,2,1,0:T(8,128)(2,1)S(1)} %bitcast.21), channel_id=1, source_target_pairs={{0,56},{4,60},{8,48},{12,52},{16,40},{20,44},{24,32},{28,36},{32,2... | collective-permute-start | bytes 49160 | tf_op jit(solution)/shard_map/ppermute | solution.py:279
  9.6 4.4 %collective-permute-start.1 = (bf16[2,2,16,256]{3,2,1,0:T(8,128)(2,1)S(1)}, bf16[2,2,16,256]{3,2,1,0:T(8,128)(2,1)S(1)}, u32[]{:S(2)}, u32[]{:S(2)}) collective-permute-start(bf16[2,2,16,256]{3,2,1,0:T(8,128)(2,1)S(1)} %pad_maximum_fusion.4), channel_id=1, source_target_pairs={{0,16},{4,20},{8,24},{12,28},{16,0},{20,4},{24,8},{28,12},{32,48},... | collective-permute-start | bytes 98312 | tf_op jit(solution)/shard_map/ppermute | solution.py:279
  14.1 3.3 %collective-permute-start.2 = (bf16[4,2,16,256]{3,2,1,0:T(8,128)(2,1)S(1)}, bf16[4,2,16,256]{3,2,1,0:T(8,128)(2,1)S(1)}, u32[]{:S(2)}, u32[]{:S(2)}) collective-permute-start(bf16[4,2,16,256]{3,2,1,0:T(8,128)(2,1)S(1)} %pad_maximum_fusion.3), channel_id=1, source_target_pairs={{0,8},{4,12},{8,0},{12,4},{16,24},{20,28},{24,16},{28,20},{32,40},... | collective-permute-start | bytes 196616 | tf_op jit(solution)/shard_map/ppermute | solution.py:279
  17.4 5.5 %collective-permute-start.3 = (bf16[8,2,16,256]{3,2,1,0:T(8,128)(2,1)S(1)}, bf16[8,2,16,256]{3,2,1,0:T(8,128)(2,1)S(1)}, u32[]{:S(2)}, u32[]{:S(2)}) collective-permute-start(bf16[8,2,16,256]{3,2,1,0:T(8,128)(2,1)S(1)} %get-tuple-element.20), channel_id=1, source_target_pairs={{0,64},{4,68},{8,72},{12,76},{16,80},{20,84},{24,88},{28,92},{32,9... | collective-permute-start | bytes 393224 | tf_op jit(solution)/shard_map/ppermute | solution.py:279
  18.7 5.0 %collective-permute-start.4 = (bf16[8,2,16,256]{3,2,1,0:T(8,128)(2,1)S(1)}, bf16[8,2,16,256]{3,2,1,0:T(8,128)(2,1)S(1)}, u32[]{:S(2)}, u32[]{:S(2)}) collective-permute-start(bf16[8,2,16,256]{3,2,1,0:T(8,128)(2,1)S(1)} %get-tuple-element.20), channel_id=1, source_target_pairs={{0,192},{4,196},{8,200},{12,204},{16,208},{20,212},{24,216},{28,22... | collective-permute-start | bytes 393224 | tf_op jit(solution)/shard_map/ppermute | solution.py:279
  23.7 9.4 %collective-permute-start.6 = (bf16[8,2,16,256]{3,2,1,0:T(8,128)(2,1)S(1)}, bf16[8,2,16,256]{3,2,1,0:T(8,128)(2,1)S(1)}, u32[]{:S(2)}, u32[]{:S(2)}) collective-permute-start(bf16[8,2,16,256]{3,2,1,0:T(8,128)(2,1)S(1)} %get-tuple-element.17), channel_id=1, source_target_pairs={{0,4},{4,0},{8,12},{12,8},{16,20},{20,16},{24,28},{28,24},{32,36},... | collective-permute-start | bytes 393224 | tf_op jit(solution)/shard_map/ppermute | solution.py:279
  28.1 4.9 %collective-permute-start.7 = (bf16[8,2,16,256]{3,2,1,0:T(8,128)(2,1)S(1)}, bf16[8,2,16,256]{3,2,1,0:T(8,128)(2,1)S(1)}, u32[]{:S(2)}, u32[]{:S(2)}) collective-permute-start(bf16[8,2,16,256]{3,2,1,0:T(8,128)(2,1)S(1)} %get-tuple-element.18), channel_id=1, source_target_pairs={{0,4},{4,0},{8,12},{12,8},{16,20},{20,16},{24,28},{28,24},{32,36},... | collective-permute-start | bytes 393224 | tf_op jit(solution)/shard_map/ppermute | solution.py:279
  28.1 5.8 %collective-permute-start.5 = (bf16[8,2,16,256]{3,2,1,0:T(8,128)(2,1)S(1)}, bf16[8,2,16,256]{3,2,1,0:T(8,128)(2,1)S(1)}, u32[]{:S(2)}, u32[]{:S(2)}) collective-permute-start(bf16[8,2,16,256]{3,2,1,0:T(8,128)(2,1)S(1)} %get-tuple-element.17), channel_id=1, source_target_pairs={{0,192},{4,196},{8,200},{12,204},{16,208},{20,212},{24,216},{28,22... | collective-permute-start | bytes 393224 | tf_op jit(solution)/shard_map/ppermute | solution.py:279
  30.0 5.4 %collective-permute-start.8 = (bf16[8,2,16,256]{3,2,1,0:T(8,128)(2,1)S(1)}, bf16[8,2,16,256]{3,2,1,0:T(8,128)(2,1)S(1)}, u32[]{:S(2)}, u32[]{:S(2)}) collective-permute-start(bf16[8,2,16,256]{3,2,1,0:T(8,128)(2,1)S(1)} %get-tuple-element.20), channel_id=1, source_target_pairs={{0,4},{4,0},{8,12},{12,8},{16,20},{20,16},{24,28},{28,24},{32,36},... | collective-permute-start | bytes 393224 | tf_op jit(solution)/shard_map/ppermute | solution.py:279
  33.9 2.3 %collective-permute-start.9 = (bf16[8,2,16,256]{3,2,1,0:T(8,128)(2,1)S(1)}, bf16[8,2,16,256]{3,2,1,0:T(8,128)(2,1)S(1)}, u32[]{:S(2)}, u32[]{:S(2)}) collective-permute-start(bf16[8,2,16,256]{3,2,1,0:T(8,128)(2,1)S(1)} %tie.9.refs_1_), channel_id=1, source_target_pairs={{0,4},{4,0},{8,12},{12,8},{16,20},{20,16},{24,28},{28,24},{32,36},... | collective-permute-start | bytes 393224 | tf_op jit(solution)/shard_map/ppermute | solution.py:279
  39.6 8.3 %collective-permute-start.11 = (bf16[2,256,256]{2,1,0:T(8,128)(2,1)S(1)}, bf16[2,256,256]{2,1,0:T(8,128)(2,1)S(1)}, u32[]{:S(2)}, u32[]{:S(2)}) collective-permute-start(bf16[2,256,256]{2,1,0:T(8,128)(2,1)S(1)} %partial.7), channel_id=1, source_target_pairs={{0,3},{1,2},{2,1},{3,0},{4,5},{5,4},{6,7},{7,6},{8,11},{9,10},{10,... | collective-permute-start | bytes 786440 | tf_op jit(solution)/shard_map/ppermute | solution.py:290
  44.3 10.0 %collective-permute-start.10 = (bf16[2,256,256]{2,1,0:T(8,128)(2,1)S(1)}, bf16[2,256,256]{2,1,0:T(8,128)(2,1)S(1)}, u32[]{:S(2)}, u32[]{:S(2)}) collective-permute-start(bf16[2,256,256]{2,1,0:T(8,128)(2,1)S(1)} %partial.5), channel_id=1, source_target_pairs={{0,3},{1,2},{2,1},{3,0},{4,5},{5,4},{6,7},{7,6},{8,11},{9,10},{10,... | collective-permute-start | bytes 786440 | tf_op jit(solution)/shard_map/ppermute | solution.py:290
  48.0 8.2 %collective-permute-start.12 = (bf16[2,256,256]{2,1,0:T(8,128)(2,1)S(1)}, bf16[2,256,256]{2,1,0:T(8,128)(2,1)S(1)}, u32[]{:S(2)}, u32[]{:S(2)}) collective-permute-start(bf16[2,256,256]{2,1,0:T(8,128)(2,1)S(1)} %add.3), channel_id=1, source_target_pairs={{0,1},{1,0},{2,3},{3,2},{4,7},{5,6},{6,5},{7,4},{8,9},{9,8},{10,11... | collective-permute-start | bytes 786440 | tf_op jit(solution)/shard_map/ppermute | solution.py:290

commit v4 on v3

--- a/solution.py
+++ b/solution.py
@@ -10,6 +10,7 @@
 SLOTS = 256
 NX, NZ, NC, NY = 4, 8, 2, 4
 BLOCK, HALF = 128, 512
+PIECES = ((0, 0, 512), (0, 512, 1000), (1, 0, 512), (1, 512, 1000))
 ROWS = 16
 CHUNK = NZ * NC * ROWS
 PAIRS = NX * CHUNK
@@ -96,7 +97,7 @@
     )(amplitudes, labels)
 
 
-def unweave_kernel(c, start, v_hbm, out_ref, held, sem):
+def unweave_kernel(c, start, v_hbm, _, out_ref, held, sem):
     _, rows, n = out_ref.shape
     sizes = [min(BLOCK, rows - at) for at in range(0, rows, BLOCK)]
     copies = [
@@ -118,12 +119,14 @@
         out_ref[1, at:at + size] = both[size:]
 
 
-def unweave(v, c, start, rows):
+def unweave(v, which, after):
+    c, start, stop = PIECES[which]
+    rows = stop - start
     _, _, a_count, n = v.shape
     return pl.pallas_call(
         functools.partial(unweave_kernel, c, start),
         out_shape=jax.ShapeDtypeStruct((a_count, rows, n), BF),
-        in_specs=[ANY],
+        in_specs=[ANY] * 2,
         out_specs=VMEM,
         scratch_shapes=[
             pltpu.VMEM((rows, a_count, n), BF),
@@ -134,7 +137,7 @@
             flops=8 * BLOCK * rows * n, bytes_accessed=8 * rows * n, transcendentals=0
         ),
         name="unweave",
-    )(v)
+    )(v, after)
 
 
 def tables_kernel(labels_ref, slot_ref, pack_ref, unpack_ref, orb_col_ref):
@@ -190,7 +193,7 @@
         near, last = held[2 * other:2 * other + 2]
         source = core ^ other
         for j in range(NZ):
-            zz = z ^ (7 * (j & 1)) ^ (2 * (j >> 1 & 1)) ^ (j >> 2)
+            zz = z ^ (7 * (j & 1)) ^ (j >> 1)
             at = pl.multiple_of((zz * NC + source) * ROWS, ROWS)
             for c in range(2):
                 rows_ref[c, pl.ds(at, ROWS), :] = jnp.where(rel == 2, last[j, c], near[index, j, c])
@@ -200,9 +203,11 @@
         full = dot(rows_ref[c], pack_ref[...])
         keep = orb == (pair_col ^ pick(orb, y * 2 + c))
         kept = jnp.where(keep, full, 0.0).astype(BF)
-        spread += [kept[:, :HALF], kept[:, HALF:]]
+        spread.append(kept)
     for a in range(2):
-        total = sum(dot(left, v_ref[a]) for left, v_ref in zip(spread, v_refs))
+        total = sum(
+            dot(spread[c][:, start:stop], v_ref[a]) for (c, start, stop), v_ref in zip(PIECES, v_refs)
+        )
         keep = orb == (pair_col ^ pick(orb, w * 2 + a))
         kept = jnp.where(keep, total, 0.0).astype(BF)
         out_ref[a] = dot(kept, unpack_ref[...]).astype(BF)
@@ -311,28 +316,31 @@
     )(*values, *others)
 
 
-def gather(block, beside):
+def gather(block, table, integrals):
     other = lambda x, z, c: (x, z, 1 - c)
     along_z = lambda value, bits: swap(value, lambda x, z, c: (x, z ^ bits, c))
     along_x = lambda value, bits: swap(value, lambda x, z, c: (x ^ bits, z, c))
+    piece = functools.partial(unweave, integrals)
     block = block[None]
-    for k, bits in enumerate((7, 2, 1)):
-        block = jnp.concatenate([block, *tie([along_z(block, bits)], *beside[k])])
+    block = jnp.concatenate([block, *tie([along_z(block, 7)], *table)])
+    v = [piece(0, block)]
+    block = jnp.concatenate([block, *tie([along_z(block, bits) for bits in (1, 2, 3)], *v)])
+    v += [piece(1, block)]
     sent = swap(block, other)
-    got = tie([along_x(block, bits) for bits in (1, 3)], *beside[3])
+    got = [*tie([along_x(block, 1)], *v[1:]), along_x(block, 3)]
+    v += [piece(2, got[0]), piece(3, got[0])]
     last = along_x(got[0], 3)
     got_other = [swap(value, other) for value in got]
-    (last,) = tie([last], *got_other, *beside[4])
-    return jnp.stack([block, *got]), last, jnp.stack([sent, *got_other]), swap(last, other)
+    (last,) = tie([last], *got_other, *v[2:])
+    return [jnp.stack([block, *got]), last, jnp.stack([sent, *got_other]), swap(last, other)], v
 
 
 def local(amplitudes, integrals, orbital_irrep, pair_irrep):
     n = integrals.shape[1]
     labels = jnp.concatenate([pair_irrep, orbital_irrep]).reshape(1, PAIRS + n)
-    v = [unweave(integrals, c, at, min(HALF, n - at)) for c in range(2) for at in (0, HALF)]
     packed, slot = compact(amplitudes, labels)
     table = tables(labels, slot)
-    held = gather(packed, (table, [v[0]], [v[1]], [v[2]], [v[3]]))
+    held, v = gather(packed, table, integrals)
     one, two = (3, 1), (1, 3)
     call = functools.partial(partial, held, v, labels, table)
     far = to_depth(call((2, 2)), one)

time: 57.9 us -> 57.2 us (0.988)
  waiting for transfers between devices: 4.77 us -> 4 us
    ppermute x10 -> x11, waiting for transfers between devices: 2.95 us -> 2.31 us  [swap(): lax.ppermute(value, 'wide', [(index(x, z, c), index(*partner(x, z, c))) f...]
    ppermute x10 -> x11, starting transfers between devices: 21 us -> 21 us  [swap(): lax.ppermute(value, 'wide', [(index(x, z, c), index(*partner(x, z, c))) f...]
  transfers between devices with their start and end apart: 13 -> 14, of which waited for: 5 -> 4; matrix products, arithmetic and copies ran while one was open for 0% -> 0% of each run, Pallas kernels for 35% -> 35%
where the time goes in v4:
time: 57.2 us; the launch traced here: 56.9 us
  starting transfers between devices  25.7 us (45%)
  Pallas kernels  25.2 us (44%)
  waiting for transfers between devices  4 us (7%)
  local copies, waits for them, and re-layouts  0.85 us (1%)
  other arithmetic  0.8 us (1%)
    ppermute x11, starting transfers between devices, swap(): lax.ppermute(value, 'wide', [(index(x, z, c), index(*partner(x, z, c))) f...  21 us
    pallas_call x4, Pallas kernels, partial(): pl.pallas_call(functools.partial(partial_kernel, turn), out_shape=jax.Sha...  13.3 us
    pallas_call x4, Pallas kernels, unweave(): pl.pallas_call(functools.partial(unweave_kernel, c, start), out_shape=jax...  9.29 us
    ppermute x3, starting transfers between devices, to_depth(): lax.ppermute(value, ('wide', 'depth'), [(w * NY + y, w * NY + (y ^ turn[w...  4.68 us
    ppermute x11, waiting for transfers between devices, swap(): lax.ppermute(value, 'wide', [(index(x, z, c), index(*partner(x, z, c))) f...  2.31 us
    ppermute x3, waiting for transfers between devices, to_depth(): lax.ppermute(value, ('wide', 'depth'), [(w * NY + y, w * NY + (y ^ turn[w...  1.69 us
    pallas_call x1, Pallas kernels, finish(): pl.pallas_call(finish_kernel, out_shape=jax.ShapeDtypeStruct(shape, BF),...  1.34 us
  transfers between devices with their start and end apart: 14, of which 4 were waited for; matrix products, arithmetic and copies ran while one was open for 0% of the time, Pallas kernels for 35%

profile of v4, /device:TPU:1, one launch (start us, length us, event | category | flops | bytes accessed | tf_op | source)
XLA Modules:
  0.0 56.9 jit_solution(3896073047856260981)
XLA Ops:
  0.7 0.8 %copy-done = bf16[16,2,1000]{2,1,0:T(2,128)(2,1)S(1)} copy-done((bf16[16,2,1000]{2,1,0:T(2,128)(2,1)S(1)}, bf16[16,2,1000]{2,1,0:T(2,128)(2,1)}, u32[]{:S(2)}) %copy-start) | copy-done | bytes 64024
  2.1 6.4 %collective-permute-start = (bf16[1,2,16,256]{3,2,1,0:T(8,128)(2,1)S(1)}, bf16[1,2,16,256]{3,2,1,0:T(8,128)(2,1)S(1)}, u32[]{:S(2)}, u32[]{:S(2)}) collective-permute-start(bf16[1,2,16,256]{3,2,1,0:T(8,128)(2,1)S(1)} %bitcast.21), channel_id=1, source_target_pairs={{0,56},{4,60},{8,48},{12,52},{16,40},{20,44},{24,32},{28,36},{32,2... | collective-permute-start | bytes 49160 | tf_op jit(solution)/shard_map/ppermute | solution.py:284
  8.5 0.7 %tables.1 = (bf16[256,1000]{1,0:T(8,128)(2,1)S(1)}, bf16[1000,256]{1,0:T(8,128)(2,1)S(1)}, s32[1000,128]{1,0:T(8,128)S(1)}) custom-call(s32[1,2024]{1,0:T(1,128)S(1)} %bitcast.15, s32[1,1000]{1,0:T(1,128)S(1)} %get-tuple-element.14.slot_ref), custom_call_target="tpu_custom_call" | custom-call | tf_op jit(solution)/shard_map/tables/pallas_call | solution.py:154
  9.6 1.6 %collective-permute-start.1 = (bf16[2,2,16,256]{3,2,1,0:T(8,128)(2,1)S(1)}, bf16[2,2,16,256]{3,2,1,0:T(8,128)(2,1)S(1)}, u32[]{:S(2)}, u32[]{:S(2)}) collective-permute-start(bf16[2,2,16,256]{3,2,1,0:T(8,128)(2,1)S(1)} %pad_maximum_fusion.2._), channel_id=1, source_target_pairs={{0,8},{4,12},{8,0},{12,4},{16,24},{20,28},{24,16},{28,20},{32,40},... | collective-permute-start | bytes 98312 | tf_op jit(solution)/shard_map/ppermute | solution.py:284
  11.8 1.6 %collective-permute-start.3 = (bf16[2,2,16,256]{3,2,1,0:T(8,128)(2,1)S(1)}, bf16[2,2,16,256]{3,2,1,0:T(8,128)(2,1)S(1)}, u32[]{:S(2)}, u32[]{:S(2)}) collective-permute-start(bf16[2,2,16,256]{3,2,1,0:T(8,128)(2,1)S(1)} %pad_maximum_fusion.2._), channel_id=1, source_target_pairs={{0,24},{4,28},{8,16},{12,20},{16,8},{20,12},{24,0},{28,4},{32,56},... | collective-permute-start | bytes 98312 | tf_op jit(solution)/shard_map/ppermute | solution.py:284
  13.4 2.3 %unweave.4.refs_3_.refs_4_ = bf16[2,512,1000]{2,1,0:T(8,128)(2,1)S(1)} custom-call(bf16[2,1000,2,1000]{3,2,1,0:T(2,128)(2,1)} %v_hbm.7, bf16[2,2,16,256]{3,2,1,0:T(8,128)(2,1)S(1)} %pad_maximum_fusion.2._), custom_call_target="tpu_custom_call" | custom-call | flops 524288000 | bytes 4096000 | tf_op jit(solution)/shard_map/unweave/pallas_call | solution.py:126
  15.8 0.9 %collective-permute-done.3.refs_2_ = bf16[2,2,16,256]{3,2,1,0:T(8,128)(2,1)S(1)} collective-permute-done((bf16[2,2,16,256]{3,2,1,0:T(8,128)(2,1)S(1)}, bf16[2,2,16,256]{3,2,1,0:T(8,128)(2,1)S(1)}, u32[]{:S(2)}, u32[]{:S(2)}) %collective-permute-start.3) | collective-permute-done | bytes 32800 | tf_op jit(solution)/shard_map/ppermute | solution.py:284
  16.7 1.3 %collective-permute-start.4 = (bf16[8,2,16,256]{3,2,1,0:T(8,128)(2,1)S(1)}, bf16[8,2,16,256]{3,2,1,0:T(8,128)(2,1)S(1)}, u32[]{:S(2)}, u32[]{:S(2)}) collective-permute-start(bf16[8,2,16,256]{3,2,1,0:T(8,128)(2,1)S(1)} %constant_dynamic-update-slice_fusion._), channel_id=1, source_target_pairs={{0,64},{4,68},{8,72},{12,76},{16,80},{20,84},{24,88},{28,92},{32,9... | collective-permute-start | bytes 393224 | tf_op jit(solution)/shard_map/ppermute | solution.py:284
  18.0 1.8 %collective-permute-start.5 = (bf16[8,2,16,256]{3,2,1,0:T(8,128)(2,1)S(1)}, bf16[8,2,16,256]{3,2,1,0:T(8,128)(2,1)S(1)}, u32[]{:S(2)}, u32[]{:S(2)}) collective-permute-start(bf16[8,2,16,256]{3,2,1,0:T(8,128)(2,1)S(1)} %constant_dynamic-update-slice_fusion._), channel_id=1, source_target_pairs={{0,192},{4,196},{8,200},{12,204},{16,208},{20,212},{24,216},{28,22... | collective-permute-start | bytes 393224 | tf_op jit(solution)/shard_map/ppermute | solution.py:284
  19.8 2.3 %unweave.5.refs_1_.refs_5_ = bf16[2,488,1000]{2,1,0:T(8,128)(2,1)S(1)} custom-call(bf16[2,1000,2,1000]{3,2,1,0:T(2,128)(2,1)} %v_hbm.7, bf16[8,2,16,256]{3,2,1,0:T(8,128)(2,1)S(1)} %constant_dynamic-update-slice_fusion._), custom_call_target="tpu_custom_call" | custom-call | flops 499712000 | bytes 3904000 | tf_op jit(solution)/shard_map/unweave/pallas_call | solution.py:126
  22.2 3.4 %collective-permute-start.7 = (bf16[8,2,16,256]{3,2,1,0:T(8,128)(2,1)S(1)}, bf16[8,2,16,256]{3,2,1,0:T(8,128)(2,1)S(1)}, u32[]{:S(2)}, u32[]{:S(2)}) collective-permute-start(bf16[8,2,16,256]{3,2,1,0:T(8,128)(2,1)S(1)} %tie.6._), channel_id=1, source_target_pairs={{0,4},{4,0},{8,12},{12,8},{16,20},{20,16},{24,28},{28,24},{32,36},... | collective-permute-start | bytes 393224 | tf_op jit(solution)/shard_map/ppermute | solution.py:284
  25.6 1.7 %collective-permute-start.8 = (bf16[8,2,16,256]{3,2,1,0:T(8,128)(2,1)S(1)}, bf16[8,2,16,256]{3,2,1,0:T(8,128)(2,1)S(1)}, u32[]{:S(2)}, u32[]{:S(2)}) collective-permute-start(bf16[8,2,16,256]{3,2,1,0:T(8,128)(2,1)S(1)} %collective-permute-done.5), channel_id=1, source_target_pairs={{0,4},{4,0},{8,12},{12,8},{16,20},{20,16},{24,28},{28,24},{32,36},... | collective-permute-start | bytes 393224 | tf_op jit(solution)/shard_map/ppermute | solution.py:284
  27.2 1.8 %collective-permute-start.6 = (bf16[8,2,16,256]{3,2,1,0:T(8,128)(2,1)S(1)}, bf16[8,2,16,256]{3,2,1,0:T(8,128)(2,1)S(1)}, u32[]{:S(2)}, u32[]{:S(2)}) collective-permute-start(bf16[8,2,16,256]{3,2,1,0:T(8,128)(2,1)S(1)} %tie.6._), channel_id=1, source_target_pairs={{0,192},{4,196},{8,200},{12,204},{16,208},{20,212},{24,216},{28,22... | collective-permute-start | bytes 393224 | tf_op jit(solution)/shard_map/ppermute | solution.py:284
  29.3 2.3 %unweave.6.refs_3_.refs_6_ = bf16[2,512,1000]{2,1,0:T(8,128)(2,1)S(1)} custom-call(bf16[2,1000,2,1000]{3,2,1,0:T(2,128)(2,1)} %v_hbm.7, bf16[8,2,16,256]{3,2,1,0:T(8,128)(2,1)S(1)} %tie.6._), custom_call_target="tpu_custom_call" | custom-call | flops 524288000 | bytes 4096000 | tf_op jit(solution)/shard_map/unweave/pallas_call | solution.py:126
  31.7 2.3 %unweave.7.refs_4_.refs_7_ = bf16[2,488,1000]{2,1,0:T(8,128)(2,1)S(1)} custom-call(bf16[2,1000,2,1000]{3,2,1,0:T(2,128)(2,1)} %v_hbm.7, bf16[8,2,16,256]{3,2,1,0:T(8,128)(2,1)S(1)} %tie.6._), custom_call_target="tpu_custom_call" | custom-call | flops 499712000 | bytes 3904000 | tf_op jit(solution)/shard_map/unweave/pallas_call | solution.py:126
  34.6 1.0 %collective-permute-done.10.refs_3_ = bf16[8,2,16,256]{3,2,1,0:T(8,128)(2,1)S(1)} collective-permute-done((bf16[8,2,16,256]{3,2,1,0:T(8,128)(2,1)S(1)}, bf16[8,2,16,256]{3,2,1,0:T(8,128)(2,1)S(1)}, u32[]{:S(2)}, u32[]{:S(2)}) %collective-permute-start.10) | collective-permute-done | bytes 131104 | tf_op jit(solution)/shard_map/ppermute | solution.py:284
  35.6 3.3 %partial.7 = bf16[2,256,256]{2,1,0:T(8,128)(2,1)S(1)} custom-call(bf16[3,8,2,16,256]{4,3,2,1,0:T(8,128)(2,1)S(1)} %pad_maximum_fusion.refs_0_, bf16[8,2,16,256]{3,2,1,0:T(8,128)(2,1)S(1)} %tie.7.refs_1_, bf16[3,8,2,16,256]{4,3,2,1,0:T(8,128)(2,1)S(1)} %pad_maximum_fusion.1.refs_2_, bf16[8,2,16,256]{3,2,1,0:T(8,128)(2,1)S(1)} %collective-permute-done.10.refs_3_, ...), custom_call_target="tpu_custom_call" | custom-call | flops 2048000000 | bytes 8000000 | tf_op jit(solution)/shard_map/partial/pallas_call | solution.py:218
  39.0 1.4 %collective-permute-start.12 = (bf16[2,256,256]{2,1,0:T(8,128)(2,1)S(1)}, bf16[2,256,256]{2,1,0:T(8,128)(2,1)S(1)}, u32[]{:S(2)}, u32[]{:S(2)}) collective-permute-start(bf16[2,256,256]{2,1,0:T(8,128)(2,1)S(1)} %partial.7), channel_id=1, source_target_pairs={{0,3},{1,2},{2,1},{3,0},{4,5},{5,4},{6,7},{7,6},{8,11},{9,10},{10,... | collective-permute-start | bytes 786440 | tf_op jit(solution)/shard_map/ppermute | solution.py:295
  40.4 3.3 %partial.5 = bf16[2,256,256]{2,1,0:T(8,128)(2,1)S(1)} custom-call(bf16[3,8,2,16,256]{4,3,2,1,0:T(8,128)(2,1)S(1)} %pad_maximum_fusion.refs_0_, bf16[8,2,16,256]{3,2,1,0:T(8,128)(2,1)S(1)} %tie.7.refs_1_, bf16[3,8,2,16,256]{4,3,2,1,0:T(8,128)(2,1)S(1)} %pad_maximum_fusion.1.refs_2_, bf16[8,2,16,256]{3,2,1,0:T(8,128)(2,1)S(1)} %collective-permute-done.10.refs_3_, ...), custom_call_target="tpu_custom_call" | custom-call | flops 2048000000 | bytes 8000000 | tf_op jit(solution)/shard_map/partial/pallas_call | solution.py:218
  43.9 3.3 %partial.6.left_ref = bf16[2,256,256]{2,1,0:T(8,128)(2,1)S(1)} custom-call(bf16[3,8,2,16,256]{4,3,2,1,0:T(8,128)(2,1)S(1)} %pad_maximum_fusion.refs_0_, bf16[8,2,16,256]{3,2,1,0:T(8,128)(2,1)S(1)} %tie.7.refs_1_, bf16[3,8,2,16,256]{4,3,2,1,0:T(8,128)(2,1)S(1)} %pad_maximum_fusion.1.refs_2_, bf16[8,2,16,256]{3,2,1,0:T(8,128)(2,1)S(1)} %collective-permute-done.10.refs_3_, ...), custom_call_target="tpu_custom_call" | custom-call | flops 2048000000 | bytes 8000000 | tf_op jit(solution)/shard_map/partial/pallas_call | solution.py:218
  47.4 3.0 %collective-permute-start.13 = (bf16[2,256,256]{2,1,0:T(8,128)(2,1)S(1)}, bf16[2,256,256]{2,1,0:T(8,128)(2,1)S(1)}, u32[]{:S(2)}, u32[]{:S(2)}) collective-permute-start(bf16[2,256,256]{2,1,0:T(8,128)(2,1)S(1)} %add.3), channel_id=1, source_target_pairs={{0,1},{1,0},{2,3},{3,2},{4,7},{5,6},{6,5},{7,4},{8,9},{9,8},{10,11... | collective-permute-start | bytes 786440 | tf_op jit(solution)/shard_map/ppermute | solution.py:295
  50.4 3.3 %partial.4.refs_0_ = bf16[2,256,256]{2,1,0:T(8,128)(2,1)S(1)} custom-call(bf16[3,8,2,16,256]{4,3,2,1,0:T(8,128)(2,1)S(1)} %pad_maximum_fusion.refs_0_, bf16[8,2,16,256]{3,2,1,0:T(8,128)(2,1)S(1)} %tie.7.refs_1_, bf16[3,8,2,16,256]{4,3,2,1,0:T(8,128)(2,1)S(1)} %pad_maximum_fusion.1.refs_2_, bf16[8,2,16,256]{3,2,1,0:T(8,128)(2,1)S(1)} %collective-permute-done.10.refs_3_, ...), custom_call_target="tpu_custom_call" | custom-call | flops 2048000000 | bytes 8000000 | tf_op jit(solution)/shard_map/partial/pallas_call | solution.py:218
  53.7 1.7 %collective-permute-done.13.refs_2_ = bf16[2,256,256]{2,1,0:T(8,128)(2,1)S(1)} collective-permute-done((bf16[2,256,256]{2,1,0:T(8,128)(2,1)S(1)}, bf16[2,256,256]{2,1,0:T(8,128)(2,1)S(1)}, u32[]{:S(2)}, u32[]{:S(2)}) %collective-permute-start.13) | collective-permute-done | bytes 262176 | tf_op jit(solution)/shard_map/ppermute | solution.py:295
  55.4 1.3 %finish.1 = bf16[2,1000,256]{2,1,0:T(8,128)(2,1)} custom-call(bf16[2,256,256]{2,1,0:T(8,128)(2,1)S(1)} %partial.4.refs_0_, bf16[2,256,256]{2,1,0:T(8,128)(2,1)S(1)} %collective-permute-done.11.refs_1_, bf16[2,256,256]{2,1,0:T(8,128)(2,1)S(1)} %collective-permute-done.13.refs_2_, s32[1,2024]{1,0:T(1,128)S(1)} %bitcast.20, ...), custom_call_target="tpu_custom_call" | custom-call | tf_op jit(solution)/shard_map/finish/pallas_call | solution.py:271
  (31 shorter events, 3.4 us)
Async XLA Ops:
  0.7 0.8 %copy-start = (bf16[16,2,1000]{2,1,0:T(2,128)(2,1)S(1)}, bf16[16,2,1000]{2,1,0:T(2,128)(2,1)}, u32[]{:S(2)}) copy-start(bf16[16,2,1000]{2,1,0:T(2,128)(2,1)} %t_ref.1) | copy-start | bytes 192004
  2.1 7.6 %collective-permute-start = (bf16[1,2,16,256]{3,2,1,0:T(8,128)(2,1)S(1)}, bf16[1,2,16,256]{3,2,1,0:T(8,128)(2,1)S(1)}, u32[]{:S(2)}, u32[]{:S(2)}) collective-permute-start(bf16[1,2,16,256]{3,2,1,0:T(8,128)(2,1)S(1)} %bitcast.21), channel_id=1, source_target_pairs={{0,56},{4,60},{8,48},{12,52},{16,40},{20,44},{24,32},{28,36},{32,2... | collective-permute-start | bytes 49160 | tf_op jit(solution)/shard_map/ppermute | solution.py:284
  9.6 6.2 %collective-permute-start.1 = (bf16[2,2,16,256]{3,2,1,0:T(8,128)(2,1)S(1)}, bf16[2,2,16,256]{3,2,1,0:T(8,128)(2,1)S(1)}, u32[]{:S(2)}, u32[]{:S(2)}) collective-permute-start(bf16[2,2,16,256]{3,2,1,0:T(8,128)(2,1)S(1)} %pad_maximum_fusion.2._), channel_id=1, source_target_pairs={{0,8},{4,12},{8,0},{12,4},{16,24},{20,28},{24,16},{28,20},{32,40},... | collective-permute-start | bytes 98312 | tf_op jit(solution)/shard_map/ppermute | solution.py:284
  11.3 4.5 %collective-permute-start.2 = (bf16[2,2,16,256]{3,2,1,0:T(8,128)(2,1)S(1)}, bf16[2,2,16,256]{3,2,1,0:T(8,128)(2,1)S(1)}, u32[]{:S(2)}, u32[]{:S(2)}) collective-permute-start(bf16[2,2,16,256]{3,2,1,0:T(8,128)(2,1)S(1)} %pad_maximum_fusion.2._), channel_id=1, source_target_pairs={{0,16},{4,20},{8,24},{12,28},{16,0},{20,4},{24,8},{28,12},{32,48},... | collective-permute-start | bytes 98312 | tf_op jit(solution)/shard_map/ppermute | solution.py:284
  11.8 4.9 %collective-permute-start.3 = (bf16[2,2,16,256]{3,2,1,0:T(8,128)(2,1)S(1)}, bf16[2,2,16,256]{3,2,1,0:T(8,128)(2,1)S(1)}, u32[]{:S(2)}, u32[]{:S(2)}) collective-permute-start(bf16[2,2,16,256]{3,2,1,0:T(8,128)(2,1)S(1)} %pad_maximum_fusion.2._), channel_id=1, source_target_pairs={{0,24},{4,28},{8,16},{12,20},{16,8},{20,12},{24,0},{28,4},{32,56},... | collective-permute-start | bytes 98312 | tf_op jit(solution)/shard_map/ppermute | solution.py:284
  16.7 5.4 %collective-permute-start.4 = (bf16[8,2,16,256]{3,2,1,0:T(8,128)(2,1)S(1)}, bf16[8,2,16,256]{3,2,1,0:T(8,128)(2,1)S(1)}, u32[]{:S(2)}, u32[]{:S(2)}) collective-permute-start(bf16[8,2,16,256]{3,2,1,0:T(8,128)(2,1)S(1)} %constant_dynamic-update-slice_fusion._), channel_id=1, source_target_pairs={{0,64},{4,68},{8,72},{12,76},{16,80},{20,84},{24,88},{28,92},{32,9... | collective-permute-start | bytes 393224 | tf_op jit(solution)/shard_map/ppermute | solution.py:284
  18.0 7.5 %collective-permute-start.5 = (bf16[8,2,16,256]{3,2,1,0:T(8,128)(2,1)S(1)}, bf16[8,2,16,256]{3,2,1,0:T(8,128)(2,1)S(1)}, u32[]{:S(2)}, u32[]{:S(2)}) collective-permute-start(bf16[8,2,16,256]{3,2,1,0:T(8,128)(2,1)S(1)} %constant_dynamic-update-slice_fusion._), channel_id=1, source_target_pairs={{0,192},{4,196},{8,200},{12,204},{16,208},{20,212},{24,216},{28,22... | collective-permute-start | bytes 393224 | tf_op jit(solution)/shard_map/ppermute | solution.py:284
  22.2 11.8 %collective-permute-start.7 = (bf16[8,2,16,256]{3,2,1,0:T(8,128)(2,1)S(1)}, bf16[8,2,16,256]{3,2,1,0:T(8,128)(2,1)S(1)}, u32[]{:S(2)}, u32[]{:S(2)}) collective-permute-start(bf16[8,2,16,256]{3,2,1,0:T(8,128)(2,1)S(1)} %tie.6._), channel_id=1, source_target_pairs={{0,4},{4,0},{8,12},{12,8},{16,20},{20,16},{24,28},{28,24},{32,36},... | collective-permute-start | bytes 393224 | tf_op jit(solution)/shard_map/ppermute | solution.py:284
  25.6 8.4 %collective-permute-start.8 = (bf16[8,2,16,256]{3,2,1,0:T(8,128)(2,1)S(1)}, bf16[8,2,16,256]{3,2,1,0:T(8,128)(2,1)S(1)}, u32[]{:S(2)}, u32[]{:S(2)}) collective-permute-start(bf16[8,2,16,256]{3,2,1,0:T(8,128)(2,1)S(1)} %collective-permute-done.5), channel_id=1, source_target_pairs={{0,4},{4,0},{8,12},{12,8},{16,20},{20,16},{24,28},{28,24},{32,36},... | collective-permute-start | bytes 393224 | tf_op jit(solution)/shard_map/ppermute | solution.py:284
  27.2 6.8 %collective-permute-start.6 = (bf16[8,2,16,256]{3,2,1,0:T(8,128)(2,1)S(1)}, bf16[8,2,16,256]{3,2,1,0:T(8,128)(2,1)S(1)}, u32[]{:S(2)}, u32[]{:S(2)}) collective-permute-start(bf16[8,2,16,256]{3,2,1,0:T(8,128)(2,1)S(1)} %tie.6._), channel_id=1, source_target_pairs={{0,192},{4,196},{8,200},{12,204},{16,208},{20,212},{24,216},{28,22... | collective-permute-start | bytes 393224 | tf_op jit(solution)/shard_map/ppermute | solution.py:284
  29.0 5.5 %collective-permute-start.9 = (bf16[8,2,16,256]{3,2,1,0:T(8,128)(2,1)S(1)}, bf16[8,2,16,256]{3,2,1,0:T(8,128)(2,1)S(1)}, u32[]{:S(2)}, u32[]{:S(2)}) collective-permute-start(bf16[8,2,16,256]{3,2,1,0:T(8,128)(2,1)S(1)} %constant_dynamic-update-slice_fusion._), channel_id=1, source_target_pairs={{0,4},{4,0},{8,12},{12,8},{16,20},{20,16},{24,28},{28,24},{32,36},... | collective-permute-start | bytes 393224 | tf_op jit(solution)/shard_map/ppermute | solution.py:284
  34.0 1.6 %collective-permute-start.10 = (bf16[8,2,16,256]{3,2,1,0:T(8,128)(2,1)S(1)}, bf16[8,2,16,256]{3,2,1,0:T(8,128)(2,1)S(1)}, u32[]{:S(2)}, u32[]{:S(2)}) collective-permute-start(bf16[8,2,16,256]{3,2,1,0:T(8,128)(2,1)S(1)} %tie.7.refs_1_), channel_id=1, source_target_pairs={{0,4},{4,0},{8,12},{12,8},{16,20},{20,16},{24,28},{28,24},{32,36},... | collective-permute-start | bytes 393224 | tf_op jit(solution)/shard_map/ppermute | solution.py:284
  39.0 8.3 %collective-permute-start.12 = (bf16[2,256,256]{2,1,0:T(8,128)(2,1)S(1)}, bf16[2,256,256]{2,1,0:T(8,128)(2,1)S(1)}, u32[]{:S(2)}, u32[]{:S(2)}) collective-permute-start(bf16[2,256,256]{2,1,0:T(8,128)(2,1)S(1)} %partial.7), channel_id=1, source_target_pairs={{0,3},{1,2},{2,1},{3,0},{4,5},{5,4},{6,7},{7,6},{8,11},{9,10},{10,... | collective-permute-start | bytes 786440 | tf_op jit(solution)/shard_map/ppermute | solution.py:295
  43.7 10.0 %collective-permute-start.11 = (bf16[2,256,256]{2,1,0:T(8,128)(2,1)S(1)}, bf16[2,256,256]{2,1,0:T(8,128)(2,1)S(1)}, u32[]{:S(2)}, u32[]{:S(2)}) collective-permute-start(bf16[2,256,256]{2,1,0:T(8,128)(2,1)S(1)} %partial.5), channel_id=1, source_target_pairs={{0,3},{1,2},{2,1},{3,0},{4,5},{5,4},{6,7},{7,6},{8,11},{9,10},{10,... | collective-permute-start | bytes 786440 | tf_op jit(solution)/shard_map/ppermute | solution.py:295
  47.4 8.1 %collective-permute-start.13 = (bf16[2,256,256]{2,1,0:T(8,128)(2,1)S(1)}, bf16[2,256,256]{2,1,0:T(8,128)(2,1)S(1)}, u32[]{:S(2)}, u32[]{:S(2)}) collective-permute-start(bf16[2,256,256]{2,1,0:T(8,128)(2,1)S(1)} %add.3), channel_id=1, source_target_pairs={{0,1},{1,0},{2,3},{3,2},{4,7},{5,6},{6,5},{7,4},{8,9},{9,8},{10,11... | collective-permute-start | bytes 786440 | tf_op jit(solution)/shard_map/ppermute | solution.py:295

commit v5 on v4

--- a/solution.py
+++ b/solution.py
@@ -341,7 +341,7 @@
     packed, slot = compact(amplitudes, labels)
     table = tables(labels, slot)
     held, v = gather(packed, table, integrals)
-    one, two = (3, 1), (1, 3)
+    one, two = (1, 3), (3, 1)
     call = functools.partial(partial, held, v, labels, table)
     far = to_depth(call((2, 2)), one)
     direct = to_depth(call(one), one)

time: 57.2 us -> 56.3 us (0.984)
  starting transfers between devices: 25.7 us -> 24.2 us
    ppermute x3, starting transfers between devices: 4.68 us -> 3.24 us  [to_depth(): lax.ppermute(value, ('wide', 'depth'), [(w * NY + y, w * NY + (y ^ turn[w...]
  transfers between devices with their start and end apart: 14 -> 14, of which waited for: 4 -> 4; matrix products, arithmetic and copies ran while one was open for 0% -> 0% of each run, Pallas kernels for 35% -> 36%
where the time goes in v5:
time: 56.3 us; the launch traced here: 56 us
  Pallas kernels  25.2 us (45%)
  starting transfers between devices  24.2 us (43%)
  waiting for transfers between devices  4.47 us (8%)
  local copies, waits for them, and re-layouts  0.85 us (2%)
  other arithmetic  0.8 us (1%)
    ppermute x11, starting transfers between devices, swap(): lax.ppermute(value, 'wide', [(index(x, z, c), index(*partner(x, z, c))) f...  21 us
    pallas_call x4, Pallas kernels, partial(): pl.pallas_call(functools.partial(partial_kernel, turn), out_shape=jax.Sha...  13.3 us
    pallas_call x4, Pallas kernels, unweave(): pl.pallas_call(functools.partial(unweave_kernel, c, start), out_shape=jax...  9.29 us
    ppermute x3, starting transfers between devices, to_depth(): lax.ppermute(value, ('wide', 'depth'), [(w * NY + y, w * NY + (y ^ turn[w...  3.24 us
    ppermute x11, waiting for transfers between devices, swap(): lax.ppermute(value, 'wide', [(index(x, z, c), index(*partner(x, z, c))) f...  2.31 us
    ppermute x3, waiting for transfers between devices, to_depth(): lax.ppermute(value, ('wide', 'depth'), [(w * NY + y, w * NY + (y ^ turn[w...  2.17 us
    pallas_call x1, Pallas kernels, finish(): pl.pallas_call(finish_kernel, out_shape=jax.ShapeDtypeStruct(shape, BF),...  1.34 us
  transfers between devices with their start and end apart: 14, of which 4 were waited for; matrix products, arithmetic and copies ran while one was open for 0% of the time, Pallas kernels for 36%

profile of v5, /device:TPU:1, one launch (start us, length us, event | category | flops | bytes accessed | tf_op | source)
XLA Modules:
  0.0 56.0 jit_solution(7285547628005123931)
XLA Ops:
  0.0 0.7 %pad_add_fusion = s32[2024]{0:T(1024)S(1)} fusion(s32[1000]{0:T(1024)} %param.6, s32[1024]{0:T(1024)} %param.7), kind=kLoop, calls=%fused_computation.8 | loop fusion | flops 2024 | bytes 16192 | tf_op jit(solution)/shard_map/concatenate | solution.py:340
  0.7 0.8 %copy-done = bf16[16,2,1000]{2,1,0:T(2,128)(2,1)S(1)} copy-done((bf16[16,2,1000]{2,1,0:T(2,128)(2,1)S(1)}, bf16[16,2,1000]{2,1,0:T(2,128)(2,1)}, u32[]{:S(2)}) %copy-start) | copy-done | bytes 64024
  2.1 6.4 %collective-permute-start = (bf16[1,2,16,256]{3,2,1,0:T(8,128)(2,1)S(1)}, bf16[1,2,16,256]{3,2,1,0:T(8,128)(2,1)S(1)}, u32[]{:S(2)}, u32[]{:S(2)}) collective-permute-start(bf16[1,2,16,256]{3,2,1,0:T(8,128)(2,1)S(1)} %bitcast.21), channel_id=1, source_target_pairs={{0,56},{4,60},{8,48},{12,52},{16,40},{20,44},{24,32},{28,36},{32,2... | collective-permute-start | bytes 49160 | tf_op jit(solution)/shard_map/ppermute | solution.py:284
  8.5 0.7 %tables.1 = (bf16[256,1000]{1,0:T(8,128)(2,1)S(1)}, bf16[1000,256]{1,0:T(8,128)(2,1)S(1)}, s32[1000,128]{1,0:T(8,128)S(1)}) custom-call(s32[1,2024]{1,0:T(1,128)S(1)} %bitcast.15, s32[1,1000]{1,0:T(1,128)S(1)} %get-tuple-element.14.slot_ref), custom_call_target="tpu_custom_call" | custom-call | tf_op jit(solution)/shard_map/tables/pallas_call | solution.py:154
  9.6 1.6 %collective-permute-start.1 = (bf16[2,2,16,256]{3,2,1,0:T(8,128)(2,1)S(1)}, bf16[2,2,16,256]{3,2,1,0:T(8,128)(2,1)S(1)}, u32[]{:S(2)}, u32[]{:S(2)}) collective-permute-start(bf16[2,2,16,256]{3,2,1,0:T(8,128)(2,1)S(1)} %pad_maximum_fusion.2._), channel_id=1, source_target_pairs={{0,8},{4,12},{8,0},{12,4},{16,24},{20,28},{24,16},{28,20},{32,40},... | collective-permute-start | bytes 98312 | tf_op jit(solution)/shard_map/ppermute | solution.py:284
  11.8 1.6 %collective-permute-start.3 = (bf16[2,2,16,256]{3,2,1,0:T(8,128)(2,1)S(1)}, bf16[2,2,16,256]{3,2,1,0:T(8,128)(2,1)S(1)}, u32[]{:S(2)}, u32[]{:S(2)}) collective-permute-start(bf16[2,2,16,256]{3,2,1,0:T(8,128)(2,1)S(1)} %pad_maximum_fusion.2._), channel_id=1, source_target_pairs={{0,24},{4,28},{8,16},{12,20},{16,8},{20,12},{24,0},{28,4},{32,56},... | collective-permute-start | bytes 98312 | tf_op jit(solution)/shard_map/ppermute | solution.py:284
  13.4 2.3 %unweave.4.refs_3_.refs_4_ = bf16[2,512,1000]{2,1,0:T(8,128)(2,1)S(1)} custom-call(bf16[2,1000,2,1000]{3,2,1,0:T(2,128)(2,1)} %v_hbm.7, bf16[2,2,16,256]{3,2,1,0:T(8,128)(2,1)S(1)} %pad_maximum_fusion.2._), custom_call_target="tpu_custom_call" | custom-call | flops 524288000 | bytes 4096000 | tf_op jit(solution)/shard_map/unweave/pallas_call | solution.py:126
  15.8 0.9 %collective-permute-done.3.refs_2_ = bf16[2,2,16,256]{3,2,1,0:T(8,128)(2,1)S(1)} collective-permute-done((bf16[2,2,16,256]{3,2,1,0:T(8,128)(2,1)S(1)}, bf16[2,2,16,256]{3,2,1,0:T(8,128)(2,1)S(1)}, u32[]{:S(2)}, u32[]{:S(2)}) %collective-permute-start.3) | collective-permute-done | bytes 32800 | tf_op jit(solution)/shard_map/ppermute | solution.py:284
  16.7 1.3 %collective-permute-start.4 = (bf16[8,2,16,256]{3,2,1,0:T(8,128)(2,1)S(1)}, bf16[8,2,16,256]{3,2,1,0:T(8,128)(2,1)S(1)}, u32[]{:S(2)}, u32[]{:S(2)}) collective-permute-start(bf16[8,2,16,256]{3,2,1,0:T(8,128)(2,1)S(1)} %constant_dynamic-update-slice_fusion._), channel_id=1, source_target_pairs={{0,64},{4,68},{8,72},{12,76},{16,80},{20,84},{24,88},{28,92},{32,9... | collective-permute-start | bytes 393224 | tf_op jit(solution)/shard_map/ppermute | solution.py:284
  18.0 1.8 %collective-permute-start.5 = (bf16[8,2,16,256]{3,2,1,0:T(8,128)(2,1)S(1)}, bf16[8,2,16,256]{3,2,1,0:T(8,128)(2,1)S(1)}, u32[]{:S(2)}, u32[]{:S(2)}) collective-permute-start(bf16[8,2,16,256]{3,2,1,0:T(8,128)(2,1)S(1)} %constant_dynamic-update-slice_fusion._), channel_id=1, source_target_pairs={{0,192},{4,196},{8,200},{12,204},{16,208},{20,212},{24,216},{28,22... | collective-permute-start | bytes 393224 | tf_op jit(solution)/shard_map/ppermute | solution.py:284
  19.8 2.3 %unweave.5.refs_1_.refs_5_ = bf16[2,488,1000]{2,1,0:T(8,128)(2,1)S(1)} custom-call(bf16[2,1000,2,1000]{3,2,1,0:T(2,128)(2,1)} %v_hbm.7, bf16[8,2,16,256]{3,2,1,0:T(8,128)(2,1)S(1)} %constant_dynamic-update-slice_fusion._), custom_call_target="tpu_custom_call" | custom-call | flops 499712000 | bytes 3904000 | tf_op jit(solution)/shard_map/unweave/pallas_call | solution.py:126
  22.2 3.4 %collective-permute-start.7 = (bf16[8,2,16,256]{3,2,1,0:T(8,128)(2,1)S(1)}, bf16[8,2,16,256]{3,2,1,0:T(8,128)(2,1)S(1)}, u32[]{:S(2)}, u32[]{:S(2)}) collective-permute-start(bf16[8,2,16,256]{3,2,1,0:T(8,128)(2,1)S(1)} %tie.6._), channel_id=1, source_target_pairs={{0,4},{4,0},{8,12},{12,8},{16,20},{20,16},{24,28},{28,24},{32,36},... | collective-permute-start | bytes 393224 | tf_op jit(solution)/shard_map/ppermute | solution.py:284
  25.6 1.7 %collective-permute-start.8 = (bf16[8,2,16,256]{3,2,1,0:T(8,128)(2,1)S(1)}, bf16[8,2,16,256]{3,2,1,0:T(8,128)(2,1)S(1)}, u32[]{:S(2)}, u32[]{:S(2)}) collective-permute-start(bf16[8,2,16,256]{3,2,1,0:T(8,128)(2,1)S(1)} %collective-permute-done.5), channel_id=1, source_target_pairs={{0,4},{4,0},{8,12},{12,8},{16,20},{20,16},{24,28},{28,24},{32,36},... | collective-permute-start | bytes 393224 | tf_op jit(solution)/shard_map/ppermute | solution.py:284
  27.2 1.8 %collective-permute-start.6 = (bf16[8,2,16,256]{3,2,1,0:T(8,128)(2,1)S(1)}, bf16[8,2,16,256]{3,2,1,0:T(8,128)(2,1)S(1)}, u32[]{:S(2)}, u32[]{:S(2)}) collective-permute-start(bf16[8,2,16,256]{3,2,1,0:T(8,128)(2,1)S(1)} %tie.6._), channel_id=1, source_target_pairs={{0,192},{4,196},{8,200},{12,204},{16,208},{20,212},{24,216},{28,22... | collective-permute-start | bytes 393224 | tf_op jit(solution)/shard_map/ppermute | solution.py:284
  29.3 2.3 %unweave.6.refs_3_.refs_6_ = bf16[2,512,1000]{2,1,0:T(8,128)(2,1)S(1)} custom-call(bf16[2,1000,2,1000]{3,2,1,0:T(2,128)(2,1)} %v_hbm.7, bf16[8,2,16,256]{3,2,1,0:T(8,128)(2,1)S(1)} %tie.6._), custom_call_target="tpu_custom_call" | custom-call | flops 524288000 | bytes 4096000 | tf_op jit(solution)/shard_map/unweave/pallas_call | solution.py:126
  31.7 2.3 %unweave.7.refs_4_.refs_7_ = bf16[2,488,1000]{2,1,0:T(8,128)(2,1)S(1)} custom-call(bf16[2,1000,2,1000]{3,2,1,0:T(2,128)(2,1)} %v_hbm.7, bf16[8,2,16,256]{3,2,1,0:T(8,128)(2,1)S(1)} %tie.6._), custom_call_target="tpu_custom_call" | custom-call | flops 499712000 | bytes 3904000 | tf_op jit(solution)/shard_map/unweave/pallas_call | solution.py:126
  34.6 1.0 %collective-permute-done.10.refs_3_ = bf16[8,2,16,256]{3,2,1,0:T(8,128)(2,1)S(1)} collective-permute-done((bf16[8,2,16,256]{3,2,1,0:T(8,128)(2,1)S(1)}, bf16[8,2,16,256]{3,2,1,0:T(8,128)(2,1)S(1)}, u32[]{:S(2)}, u32[]{:S(2)}) %collective-permute-start.10) | collective-permute-done | bytes 131104 | tf_op jit(solution)/shard_map/ppermute | solution.py:284
  35.6 3.3 %partial.7 = bf16[2,256,256]{2,1,0:T(8,128)(2,1)S(1)} custom-call(bf16[3,8,2,16,256]{4,3,2,1,0:T(8,128)(2,1)S(1)} %pad_maximum_fusion.refs_0_, bf16[8,2,16,256]{3,2,1,0:T(8,128)(2,1)S(1)} %tie.7.refs_1_, bf16[3,8,2,16,256]{4,3,2,1,0:T(8,128)(2,1)S(1)} %pad_maximum_fusion.1.refs_2_, bf16[8,2,16,256]{3,2,1,0:T(8,128)(2,1)S(1)} %collective-permute-done.10.refs_3_, ...), custom_call_target="tpu_custom_call" | custom-call | flops 2048000000 | bytes 8000000 | tf_op jit(solution)/shard_map/partial/pallas_call | solution.py:218
  39.0 2.8 %collective-permute-start.12 = (bf16[2,256,256]{2,1,0:T(8,128)(2,1)S(1)}, bf16[2,256,256]{2,1,0:T(8,128)(2,1)S(1)}, u32[]{:S(2)}, u32[]{:S(2)}) collective-permute-start(bf16[2,256,256]{2,1,0:T(8,128)(2,1)S(1)} %partial.7), channel_id=1, source_target_pairs={{0,1},{1,0},{2,3},{3,2},{4,7},{5,6},{6,5},{7,4},{8,9},{9,8},{10,11... | collective-permute-start | bytes 786440 | tf_op jit(solution)/shard_map/ppermute | solution.py:295
  41.8 3.3 %partial.5 = bf16[2,256,256]{2,1,0:T(8,128)(2,1)S(1)} custom-call(bf16[3,8,2,16,256]{4,3,2,1,0:T(8,128)(2,1)S(1)} %pad_maximum_fusion.refs_0_, bf16[8,2,16,256]{3,2,1,0:T(8,128)(2,1)S(1)} %tie.7.refs_1_, bf16[3,8,2,16,256]{4,3,2,1,0:T(8,128)(2,1)S(1)} %pad_maximum_fusion.1.refs_2_, bf16[8,2,16,256]{3,2,1,0:T(8,128)(2,1)S(1)} %collective-permute-done.10.refs_3_, ...), custom_call_target="tpu_custom_call" | custom-call | flops 2048000000 | bytes 8000000 | tf_op jit(solution)/shard_map/partial/pallas_call | solution.py:218
  45.2 3.3 %partial.6.left_ref = bf16[2,256,256]{2,1,0:T(8,128)(2,1)S(1)} custom-call(bf16[3,8,2,16,256]{4,3,2,1,0:T(8,128)(2,1)S(1)} %pad_maximum_fusion.refs_0_, bf16[8,2,16,256]{3,2,1,0:T(8,128)(2,1)S(1)} %tie.7.refs_1_, bf16[3,8,2,16,256]{4,3,2,1,0:T(8,128)(2,1)S(1)} %pad_maximum_fusion.1.refs_2_, bf16[8,2,16,256]{3,2,1,0:T(8,128)(2,1)S(1)} %collective-permute-done.10.refs_3_, ...), custom_call_target="tpu_custom_call" | custom-call | flops 2048000000 | bytes 8000000 | tf_op jit(solution)/shard_map/partial/pallas_call | solution.py:218
  49.0 3.3 %partial.4.refs_0_ = bf16[2,256,256]{2,1,0:T(8,128)(2,1)S(1)} custom-call(bf16[3,8,2,16,256]{4,3,2,1,0:T(8,128)(2,1)S(1)} %pad_maximum_fusion.refs_0_, bf16[8,2,16,256]{3,2,1,0:T(8,128)(2,1)S(1)} %tie.7.refs_1_, bf16[3,8,2,16,256]{4,3,2,1,0:T(8,128)(2,1)S(1)} %pad_maximum_fusion.1.refs_2_, bf16[8,2,16,256]{3,2,1,0:T(8,128)(2,1)S(1)} %collective-permute-done.10.refs_3_, ...), custom_call_target="tpu_custom_call" | custom-call | flops 2048000000 | bytes 8000000 | tf_op jit(solution)/shard_map/partial/pallas_call | solution.py:218
  52.3 2.2 %collective-permute-done.13.refs_2_ = bf16[2,256,256]{2,1,0:T(8,128)(2,1)S(1)} collective-permute-done((bf16[2,256,256]{2,1,0:T(8,128)(2,1)S(1)}, bf16[2,256,256]{2,1,0:T(8,128)(2,1)S(1)}, u32[]{:S(2)}, u32[]{:S(2)}) %collective-permute-start.13) | collective-permute-done | bytes 262176 | tf_op jit(solution)/shard_map/ppermute | solution.py:295
  54.5 1.3 %finish.1 = bf16[2,1000,256]{2,1,0:T(8,128)(2,1)} custom-call(bf16[2,256,256]{2,1,0:T(8,128)(2,1)S(1)} %partial.4.refs_0_, bf16[2,256,256]{2,1,0:T(8,128)(2,1)S(1)} %collective-permute-done.11.refs_1_, bf16[2,256,256]{2,1,0:T(8,128)(2,1)S(1)} %collective-permute-done.13.refs_2_, s32[1,2024]{1,0:T(1,128)S(1)} %bitcast.20, ...), custom_call_target="tpu_custom_call" | custom-call | tf_op jit(solution)/shard_map/finish/pallas_call | solution.py:271
  (31 shorter events, 2.8 us)
Async XLA Ops:
  0.7 0.8 %copy-start = (bf16[16,2,1000]{2,1,0:T(2,128)(2,1)S(1)}, bf16[16,2,1000]{2,1,0:T(2,128)(2,1)}, u32[]{:S(2)}) copy-start(bf16[16,2,1000]{2,1,0:T(2,128)(2,1)} %t_ref.1) | copy-start | bytes 192004
  2.1 7.6 %collective-permute-start = (bf16[1,2,16,256]{3,2,1,0:T(8,128)(2,1)S(1)}, bf16[1,2,16,256]{3,2,1,0:T(8,128)(2,1)S(1)}, u32[]{:S(2)}, u32[]{:S(2)}) collective-permute-start(bf16[1,2,16,256]{3,2,1,0:T(8,128)(2,1)S(1)} %bitcast.21), channel_id=1, source_target_pairs={{0,56},{4,60},{8,48},{12,52},{16,40},{20,44},{24,32},{28,36},{32,2... | collective-permute-start | bytes 49160 | tf_op jit(solution)/shard_map/ppermute | solution.py:284
  9.6 6.2 %collective-permute-start.1 = (bf16[2,2,16,256]{3,2,1,0:T(8,128)(2,1)S(1)}, bf16[2,2,16,256]{3,2,1,0:T(8,128)(2,1)S(1)}, u32[]{:S(2)}, u32[]{:S(2)}) collective-permute-start(bf16[2,2,16,256]{3,2,1,0:T(8,128)(2,1)S(1)} %pad_maximum_fusion.2._), channel_id=1, source_target_pairs={{0,8},{4,12},{8,0},{12,4},{16,24},{20,28},{24,16},{28,20},{32,40},... | collective-permute-start | bytes 98312 | tf_op jit(solution)/shard_map/ppermute | solution.py:284
  11.3 4.5 %collective-permute-start.2 = (bf16[2,2,16,256]{3,2,1,0:T(8,128)(2,1)S(1)}, bf16[2,2,16,256]{3,2,1,0:T(8,128)(2,1)S(1)}, u32[]{:S(2)}, u32[]{:S(2)}) collective-permute-start(bf16[2,2,16,256]{3,2,1,0:T(8,128)(2,1)S(1)} %pad_maximum_fusion.2._), channel_id=1, source_target_pairs={{0,16},{4,20},{8,24},{12,28},{16,0},{20,4},{24,8},{28,12},{32,48},... | collective-permute-start | bytes 98312 | tf_op jit(solution)/shard_map/ppermute | solution.py:284
  11.8 4.9 %collective-permute-start.3 = (bf16[2,2,16,256]{3,2,1,0:T(8,128)(2,1)S(1)}, bf16[2,2,16,256]{3,2,1,0:T(8,128)(2,1)S(1)}, u32[]{:S(2)}, u32[]{:S(2)}) collective-permute-start(bf16[2,2,16,256]{3,2,1,0:T(8,128)(2,1)S(1)} %pad_maximum_fusion.2._), channel_id=1, source_target_pairs={{0,24},{4,28},{8,16},{12,20},{16,8},{20,12},{24,0},{28,4},{32,56},... | collective-permute-start | bytes 98312 | tf_op jit(solution)/shard_map/ppermute | solution.py:284
  16.7 5.4 %collective-permute-start.4 = (bf16[8,2,16,256]{3,2,1,0:T(8,128)(2,1)S(1)}, bf16[8,2,16,256]{3,2,1,0:T(8,128)(2,1)S(1)}, u32[]{:S(2)}, u32[]{:S(2)}) collective-permute-start(bf16[8,2,16,256]{3,2,1,0:T(8,128)(2,1)S(1)} %constant_dynamic-update-slice_fusion._), channel_id=1, source_target_pairs={{0,64},{4,68},{8,72},{12,76},{16,80},{20,84},{24,88},{28,92},{32,9... | collective-permute-start | bytes 393224 | tf_op jit(solution)/shard_map/ppermute | solution.py:284
  18.0 7.5 %collective-permute-start.5 = (bf16[8,2,16,256]{3,2,1,0:T(8,128)(2,1)S(1)}, bf16[8,2,16,256]{3,2,1,0:T(8,128)(2,1)S(1)}, u32[]{:S(2)}, u32[]{:S(2)}) collective-permute-start(bf16[8,2,16,256]{3,2,1,0:T(8,128)(2,1)S(1)} %constant_dynamic-update-slice_fusion._), channel_id=1, source_target_pairs={{0,192},{4,196},{8,200},{12,204},{16,208},{20,212},{24,216},{28,22... | collective-permute-start | bytes 393224 | tf_op jit(solution)/shard_map/ppermute | solution.py:284
  22.2 11.8 %collective-permute-start.7 = (bf16[8,2,16,256]{3,2,1,0:T(8,128)(2,1)S(1)}, bf16[8,2,16,256]{3,2,1,0:T(8,128)(2,1)S(1)}, u32[]{:S(2)}, u32[]{:S(2)}) collective-permute-start(bf16[8,2,16,256]{3,2,1,0:T(8,128)(2,1)S(1)} %tie.6._), channel_id=1, source_target_pairs={{0,4},{4,0},{8,12},{12,8},{16,20},{20,16},{24,28},{28,24},{32,36},... | collective-permute-start | bytes 393224 | tf_op jit(solution)/shard_map/ppermute | solution.py:284
  25.6 8.4 %collective-permute-start.8 = (bf16[8,2,16,256]{3,2,1,0:T(8,128)(2,1)S(1)}, bf16[8,2,16,256]{3,2,1,0:T(8,128)(2,1)S(1)}, u32[]{:S(2)}, u32[]{:S(2)}) collective-permute-start(bf16[8,2,16,256]{3,2,1,0:T(8,128)(2,1)S(1)} %collective-permute-done.5), channel_id=1, source_target_pairs={{0,4},{4,0},{8,12},{12,8},{16,20},{20,16},{24,28},{28,24},{32,36},... | collective-permute-start | bytes 393224 | tf_op jit(solution)/shard_map/ppermute | solution.py:284
  27.2 6.8 %collective-permute-start.6 = (bf16[8,2,16,256]{3,2,1,0:T(8,128)(2,1)S(1)}, bf16[8,2,16,256]{3,2,1,0:T(8,128)(2,1)S(1)}, u32[]{:S(2)}, u32[]{:S(2)}) collective-permute-start(bf16[8,2,16,256]{3,2,1,0:T(8,128)(2,1)S(1)} %tie.6._), channel_id=1, source_target_pairs={{0,192},{4,196},{8,200},{12,204},{16,208},{20,212},{24,216},{28,22... | collective-permute-start | bytes 393224 | tf_op jit(solution)/shard_map/ppermute | solution.py:284
  29.0 5.5 %collective-permute-start.9 = (bf16[8,2,16,256]{3,2,1,0:T(8,128)(2,1)S(1)}, bf16[8,2,16,256]{3,2,1,0:T(8,128)(2,1)S(1)}, u32[]{:S(2)}, u32[]{:S(2)}) collective-permute-start(bf16[8,2,16,256]{3,2,1,0:T(8,128)(2,1)S(1)} %constant_dynamic-update-slice_fusion._), channel_id=1, source_target_pairs={{0,4},{4,0},{8,12},{12,8},{16,20},{20,16},{24,28},{28,24},{32,36},... | collective-permute-start | bytes 393224 | tf_op jit(solution)/shard_map/ppermute | solution.py:284
  34.0 1.6 %collective-permute-start.10 = (bf16[8,2,16,256]{3,2,1,0:T(8,128)(2,1)S(1)}, bf16[8,2,16,256]{3,2,1,0:T(8,128)(2,1)S(1)}, u32[]{:S(2)}, u32[]{:S(2)}) collective-permute-start(bf16[8,2,16,256]{3,2,1,0:T(8,128)(2,1)S(1)} %tie.7.refs_1_), channel_id=1, source_target_pairs={{0,4},{4,0},{8,12},{12,8},{16,20},{20,16},{24,28},{28,24},{32,36},... | collective-permute-start | bytes 393224 | tf_op jit(solution)/shard_map/ppermute | solution.py:284
  39.0 9.6 %collective-permute-start.12 = (bf16[2,256,256]{2,1,0:T(8,128)(2,1)S(1)}, bf16[2,256,256]{2,1,0:T(8,128)(2,1)S(1)}, u32[]{:S(2)}, u32[]{:S(2)}) collective-permute-start(bf16[2,256,256]{2,1,0:T(8,128)(2,1)S(1)} %partial.7), channel_id=1, source_target_pairs={{0,1},{1,0},{2,3},{3,2},{4,7},{5,6},{6,5},{7,4},{8,9},{9,8},{10,11... | collective-permute-start | bytes 786440 | tf_op jit(solution)/shard_map/ppermute | solution.py:295
  45.1 7.2 %collective-permute-start.11 = (bf16[2,256,256]{2,1,0:T(8,128)(2,1)S(1)}, bf16[2,256,256]{2,1,0:T(8,128)(2,1)S(1)}, u32[]{:S(2)}, u32[]{:S(2)}) collective-permute-start(bf16[2,256,256]{2,1,0:T(8,128)(2,1)S(1)} %partial.5), channel_id=1, source_target_pairs={{0,1},{1,0},{2,3},{3,2},{4,7},{5,6},{6,5},{7,4},{8,9},{9,8},{10,11... | collective-permute-start | bytes 786440 | tf_op jit(solution)/shard_map/ppermute | solution.py:295
  48.6 5.8 %collective-permute-start.13 = (bf16[2,256,256]{2,1,0:T(8,128)(2,1)S(1)}, bf16[2,256,256]{2,1,0:T(8,128)(2,1)S(1)}, u32[]{:S(2)}, u32[]{:S(2)}) collective-permute-start(bf16[2,256,256]{2,1,0:T(8,128)(2,1)S(1)} %add.3), channel_id=1, source_target_pairs={{0,3},{1,2},{2,1},{3,0},{4,5},{5,4},{6,7},{7,6},{8,11},{9,10},{10,... | collective-permute-start | bytes 786440 | tf_op jit(solution)/shard_map/ppermute | solution.py:295
